TPU v7x, 32 devices: a whole 2x2x4 slice. The times are simulated.
32 devices in a mesh: dp: 16 (over z, y, x), mp: 2 (over core).
Axes of the slice: x: 2, y: 2, z: 4, core: 2. Of those that a mesh axis runs over, the one named last changes fastest.
Arguments:
- hidden_in: float32 [6144, 960], P(('dp', 'mp')), may hold values from -6 to 6
- sel_one: int32 [32, 192], P(('dp', 'mp')), may hold values from 0 to 192, as said below
- sel_two: int32 [32, 160], P(('dp', 'mp')), may hold values from 0 to 192, as said below
- sel_three: int32 [32, 128], P(('dp', 'mp')), may hold values from 0 to 192, as said below
- segment_ids: int32 [32, 192], P(('dp', 'mp')), may hold values from 0 to 5, never falling along the last dimension, each value on 1 to 96 neighbouring positions
- pad_mask: int32 [32, 192], P(('dp', 'mp')), may hold values from 0 to 1, as said below
- qkv_weight: bfloat16 [960, 1600], replicated, may hold values from -0.1875 to 0.1875
- out_weight: bfloat16 [960, 960], replicated, may hold values from -0.375 to 0.375
- gate_weight: bfloat16 [960, 2560], P(None, 'mp'), may hold values from -0.1875 to 0.1875
- up_weight: bfloat16 [960, 2560], P(None, 'mp'), may hold values from -0.1875 to 0.1875
- down_weight: bfloat16 [960, 2560], P(None, 'mp'), may hold values from -0.125 to 0.125
- norm_one: float32 [960], replicated, may hold values from 0.5 to 1.5
- norm_two: float32 [960], replicated, may hold values from 0.5 to 1.5
- router_weight: float32 [3, 960], replicated, may hold values from -0.125 to 0.125
- d_hidden: float32 [6144, 960], P(('dp', 'mp')), may hold values from -6 to 6
Outputs:
- hidden_out: float32 [6144, 960], P(('dp', 'mp'))
- d_input: float32 [6144, 960], P(('dp', 'mp'))
- attn_weight_grads: float32 [2457600], P(('dp', 'mp'))
- ffn_weight_grads: float32 [2, 3686400], P('mp', 'dp')
- norm_one_grad: float32 [960], replicated
- norm_two_grad: float32 [960], replicated
- router_grad: float32 [3, 960], replicated
Inputs may be any that keep to these rules, and one draw needn't show every extreme that they name: `sel_one`: row s lists the positions active in recursion one for sequence s in increasing order, followed by 192 in every empty entry. Some row has no empty entry. Over the sequences placed on one index of mp, the active counts add up to 96 times the devices of dp. `sel_two`: as for sel_one, for recursion two, with 80 in place of 96. `sel_three`: as for sel_one, for recursion three, with 64 in place of 96. `pad_mask`: each row is ones followed by zeros. `segment_ids`: ids never fall along a row.
All inputs are finite; a program needn't handle non-finite values.
Results may differ from a plain program's by a relative error of at most 0.025.
Values may be sent and summed in bfloat16 or wider, within the bound.
No kernel may reach another device: no remote copies, remote signals or barrier semaphores. Data moves between devices by JAX's collectives and lax.ppermute only.
A program may use at most 256 MiB of HBM per device.

v0:
```python
import functools
import math

import jax
import jax.numpy as jnp
import numpy as np
from jax import lax
from jax.experimental import pallas as pl
from jax.experimental.pallas import tpu as pltpu
from jax.sharding import PartitionSpec as P

HEADS = 15
KV_HEADS = 5
HEAD_DIM = 64
RECURSIONS = 3
GROUPS = HEADS // KV_HEADS
EPS = 1e-05
BF = jnp.bfloat16
F32 = jnp.float32


LANES = 128
CHUNKS = -(-HEADS * HEAD_DIM // LANES)
ROWS = 32
BLOCK = 256
MIB = 1 << 20
VMEM_MIB = 63


def rotary_tables(seq_len):
    half = HEAD_DIM // 2
    frequency = np.float32(100000.0) ** (
        np.float32(-2.0) * np.arange(half, dtype=np.float32) / np.float32(HEAD_DIM)
    )
    angles = np.arange(seq_len, dtype=np.float32)[:, None] * frequency.astype(np.float32)
    cosine, sine = np.cos(angles), np.sin(angles)
    return (
        jnp.asarray(np.concatenate([cosine] * 4, axis=1), F32),
        jnp.asarray(np.concatenate([-sine, sine] * 2, axis=1), F32),
    )


def contract_rows(left, right):
    return lax.dot_general(left, right, (((0,), (0,)), ((), ())), preferred_element_type=F32)


def contract_last(left, right):
    return lax.dot_general(left, right, (((1,), (1,)), ((), ())), preferred_element_type=F32)


def plain(left, right):
    return jnp.dot(left, right, preferred_element_type=F32)


def inverse_rms(rows):
    return lax.rsqrt(jnp.mean(rows * rows, axis=-1, keepdims=True) + EPS)


def norm_back(rows, gain, d_out):
    inv = inverse_rms(rows)
    scaled = d_out * gain
    inner = jnp.mean(scaled * rows, axis=-1, keepdims=True)
    d_rows = inv * scaled - rows * (inv * inv * inv * inner)
    return d_rows, jnp.sum(d_out * rows * inv, axis=0, keepdims=True)


def lane_of(rows):
    return lax.broadcasted_iota(jnp.int32, (rows, LANES), 1)


def swapped(chunk):
    first = lane_of(chunk.shape[0]) % HEAD_DIM < HEAD_DIM // 2
    return jnp.where(first, pltpu.roll(chunk, LANES - 32, 1), pltpu.roll(chunk, 32, 1))


def other_half(chunk):
    return pltpu.roll(chunk, HEAD_DIM, 1)


def over_rows(count, body):
    def lap(i, carry):
        body(pl.ds(pl.multiple_of(i * ROWS, ROWS), ROWS))
        return carry

    lax.fori_loop(0, count // ROWS, lap, 0)


def attention_forward(x_ref, bias_ref, cos_ref, sin_ref, gain, qkv_w, n1_ref, q_ref, kz_ref, vz_ref, p_ref, o_ref):
    seq_len, width = x_ref.shape
    scale = 1.0 / math.sqrt(HEAD_DIM)

    def norm(rows):
        x = x_ref[rows, :]
        n1_ref[rows, :] = (x * inverse_rms(x) * gain).astype(BF)

    over_rows(seq_len, norm)
    lower = lane_of(seq_len) < HEAD_DIM
    n1 = n1_ref[...]

    def spread(ref, head, chunk, upper):
        flipped = other_half(chunk)
        here, there = (flipped, chunk) if upper else (chunk, flipped)
        ref[2 * head] = jnp.where(lower, here, 0.0).astype(BF)
        ref[2 * head + 1] = jnp.where(lower, 0.0, there).astype(BF)

    columns = qkv_w.shape[1]
    for start in range(0, columns, 2 * LANES):
        wide = plain(n1, qkv_w[:, start : min(start + 2 * LANES, columns)])
        for part in range(0, wide.shape[1], LANES):
            chunk = wide[:, part : part + LANES]
            if chunk.shape[1] < LANES:
                chunk = jnp.concatenate([chunk, jnp.zeros_like(chunk)], axis=1)
            at = (start + part) // LANES
            heads = (2 * at, 2 * at + 1)
            if heads[0] < HEADS + KV_HEADS:
                chunk = chunk * cos_ref[...] + swapped(chunk) * sin_ref[...]
                if heads[0] < HEADS:
                    q_ref[:, at * LANES : (at + 1) * LANES] = chunk.astype(BF)
            for upper, head in enumerate(heads):
                if HEADS <= head < HEADS + KV_HEADS:
                    spread(kz_ref, head - HEADS, chunk, upper)
                elif HEADS + KV_HEADS <= head < HEADS + 2 * KV_HEADS:
                    spread(vz_ref, head - HEADS - KV_HEADS, chunk, upper)

    for at in range(CHUNKS):
        query = q_ref[:, at * LANES : (at + 1) * LANES]
        total = None
        for upper in range(2):
            head = 2 * at + upper
            if head < HEADS:
                key = 2 * (head // GROUPS) + upper
                scores = contract_last(query, kz_ref[key]) * scale + bias_ref[...]
                top = jnp.max(scores, axis=-1, keepdims=True)
                exponent = jnp.exp(scores - top)
                share = pl.reciprocal(jnp.sum(exponent, axis=-1, keepdims=True))
                attend = (exponent * share).astype(BF)
                p_ref[head] = attend
                mixed = plain(attend, vz_ref[key])
                total = mixed if total is None else total + mixed
        stop = min(width, (at + 1) * LANES)
        o_ref[:, at * LANES : stop] = total[:, : stop - at * LANES].astype(BF)


def attention_out(x_ref, o_ref, out_w, gain, attn_ref, n2_ref):
    attn_ref[...] = plain(o_ref[...], out_w[...])

    def norm(rows):
        after = x_ref[rows, :] + attn_ref[rows, :]
        n2_ref[rows, :] = (after * inverse_rms(after) * gain).astype(BF)

    over_rows(x_ref.shape[0], norm)


def feed_forward(n2_ref, sides, f_ref):
    n2 = n2_ref[...]
    for side, (gate_w, up_w, down_w, m_ref, slope_ref, silu_ref) in enumerate(sides):
        for start in range(0, gate_w.shape[1], BLOCK):
            at = slice(start, start + BLOCK)
            g, u = plain(n2, gate_w[:, at]), plain(n2, up_w[:, at])
            s = jax.nn.sigmoid(g)
            silu = g * s
            m_ref[:, at] = (silu * u).astype(BF)
            slope_ref[:, at] = (u * s * (1.0 + g * (1.0 - s))).astype(BF)
            silu_ref[:, at] = silu.astype(BF)
        part = contract_last(m_ref[...], down_w[...])
        f_ref[...] = part if side == 0 else f_ref[...] + part


def feed_backward(df_ref, sides, d_two_ref):
    d_feed = df_ref[...]
    for side, (gate_w, up_w, down_w, slope_ref, silu_ref, dg_ref, du_ref) in enumerate(sides):
        for start in range(0, gate_w.shape[1], BLOCK):
            at = slice(start, start + BLOCK)
            d_hidden = plain(d_feed, down_w[:, at])
            dg_ref[:, at] = (d_hidden * slope_ref[:, at].astype(F32)).astype(BF)
            du_ref[:, at] = (d_hidden * silu_ref[:, at].astype(F32)).astype(BF)
        part = contract_last(dg_ref[...], gate_w[...]) + contract_last(du_ref[...], up_w[...])
        d_two_ref[...] = part if side == 0 else d_two_ref[...] + part


def attention_backward(d_attn_ref, out_w, qkv_w, cos_ref, sin_ref, q_ref, kz_ref, vz_ref, p_ref, do_ref, du_ref):
    seq_len, width = d_attn_ref.shape
    scale = 1.0 / math.sqrt(HEAD_DIM)
    do_ref[:, :width] = contract_last(d_attn_ref[...], out_w[...]).astype(BF)
    do_ref[:, width:] = jnp.zeros((seq_len, do_ref.shape[1] - width), BF)
    lower = lane_of(seq_len) < HEAD_DIM
    cosine, sine = cos_ref[...], sin_ref[...]

    def back(chunk):
        chunk = chunk * scale
        return chunk * cosine - swapped(chunk) * sine

    waiting, d_k, d_v = None, {}, {}
    sums = [[None, None], [None, None]]
    for at in range(CHUNKS):
        query, d_mixed = (ref[:, at * LANES : (at + 1) * LANES] for ref in (q_ref, do_ref))
        d_query = None
        for upper in range(2):
            head = 2 * at + upper
            if head >= HEADS:
                continue
            group = head // GROUPS
            key = 2 * group + upper
            attend = p_ref[head]
            d_attend = contract_last(d_mixed, vz_ref[key])
            soft = attend.astype(F32)
            weighted = soft * d_attend
            inner = jnp.sum(weighted, axis=-1, keepdims=True)
            d_scores = (weighted - soft * inner).astype(BF)
            part = plain(d_scores, kz_ref[key])
            d_query = part if d_query is None else d_query + part
            for which, term in ((0, contract_rows(d_scores, query)), (1, contract_rows(attend, d_mixed))):
                old = sums[which][upper]
                sums[which][upper] = term if old is None else old + term
            if head % GROUPS == GROUPS - 1:
                for which, store in ((0, d_k), (1, d_v)):
                    both = jnp.where(lower, sums[which][0], sums[which][1])
                    store[group] = both + other_half(both)
                sums = [[None, None], [None, None]]
        if at < CHUNKS - 1:
            du_ref[:, at * LANES : (at + 1) * LANES] = back(d_query).astype(BF)
        else:
            waiting = d_query
    tail = jnp.where(lower, waiting, d_k[0])
    du_ref[:, (CHUNKS - 1) * LANES : CHUNKS * LANES] = back(tail).astype(BF)
    for i in range(2):
        at = CHUNKS + i
        du_ref[:, at * LANES : (at + 1) * LANES] = back(jnp.where(lower, d_k[1 + 2 * i], d_k[2 + 2 * i])).astype(BF)
        at = CHUNKS + 2 + i
        du_ref[:, at * LANES : (at + 1) * LANES] = jnp.where(lower, d_v[2 * i], d_v[2 * i + 1]).astype(BF)
    at = CHUNKS + 4
    du_ref[:, at * LANES :] = d_v[4][:, : du_ref.shape[1] - at * LANES].astype(BF)


def router_gate(x, router_row):
    return jax.nn.sigmoid(jnp.sum(x * router_row, axis=-1, keepdims=True))


def masks(select_refs, segment_ref, pad_ref, bias_ref, active_ref):
    seq_len = segment_ref.shape[1]
    square = (seq_len, seq_len)
    query, key = (lax.broadcasted_iota(jnp.int32, square, axis) for axis in (0, 1))
    diagonal = query == key
    segment = segment_ref[...].astype(F32)
    own = jnp.sum(jnp.where(diagonal, segment, 0.0), axis=1, keepdims=True)
    near = (key <= query) & (segment == own)
    real = pad_ref[...] == 1
    for recursion, ref in enumerate(select_refs):
        place = lax.broadcasted_iota(jnp.int32, (seq_len, ref.shape[1]), 0)
        active = jnp.max(jnp.where(ref[...] == place, 1.0, 0.0), axis=1, keepdims=True)
        active_ref[recursion] = active
        along = jnp.sum(jnp.where(diagonal, active, 0.0), axis=0, keepdims=True)
        usable = (along > 0.0) & real
        bias_ref[recursion] = jnp.where(near & (usable | diagonal), 0.0, -1e30)


def first_attention(x_ref, sel_one, sel_two, sel_three, segment_ref, pad_ref, cos_ref, sin_ref, gain_one, gain_two, qkv_w, out_w,
                    n1_ref, q_ref, kz_ref, vz_ref, p_ref, o_ref, attn_ref, n2_ref, bias_ref, active_ref):
    n1, o = n1_ref.at[0], o_ref.at[0]
    masks((sel_one, sel_two, sel_three), segment_ref, pad_ref, bias_ref, active_ref)
    attention_forward(x_ref, bias_ref.at[0], cos_ref, sin_ref, gain_one[...], qkv_w, n1, q_ref, kz_ref, vz_ref, p_ref, o)
    attention_out(x_ref, o, out_w, gain_two[...], attn_ref, n2_ref)


def load_all(pairs, sems):
    copies = [pltpu.make_async_copy(src, dst, sems.at[i]) for i, (src, dst) in enumerate(pairs)]
    return copies


def forward_steps(x0_ref, attn0_ref, n20_ref, bias_ref, active_ref, router_ref, cos_ref, sin_ref, gain_one, gain_two,
                  n1_in, o_in, qkv_hbm, out_hbm, *rest):
    feed_hbm, rest = rest[:6], rest[6:]
    (n1_ref, o_ref, q_ref, kz_ref, vz_ref, p_ref, x_ref, a_ref, branch_ref, n2_ref,
     m0, m1, slope0, slope1, silu0, silu1, final_ref), rest = rest[:17], rest[17:]
    qkv_w, out_w, w0, w1, w2, w3, w4, w5, state, attn, n2, total, sems = rest
    step = pl.program_id(0)
    copies = load_all(list(zip((*feed_hbm, qkv_hbm, out_hbm), (w0, w1, w2, w3, w4, w5, qkv_w, out_w))), sems)

    @pl.when(step == 0)
    def _():
        for copy in copies:
            copy.start()
        state[...] = x0_ref[...]
        attn[...] = attn0_ref[...]
        n2[...] = n20_ref[...]
        for copy in copies[:6]:
            copy.wait()

    n2_ref[0] = n2[...]
    feed_forward(n2, ((w0, w1, w2, m0.at[0], slope0.at[0], silu0.at[0]), (w3, w4, w5, m1.at[0], slope1.at[0], silu1.at[0])), total)
    router_row = router_ref[pl.ds(step, 1), :]

    def finish(rows):
        x, attn_rows = state[rows, :], attn[rows, :]
        x_ref[0, rows, :] = x
        a_ref[0, rows, :] = x + attn_rows
        branch = attn_rows + total[rows, :].astype(BF).astype(F32)
        branch_ref[0, rows, :] = branch
        new = jnp.where(active_ref[0, rows, :] > 0, x + router_gate(x, router_row) * branch, x)
        state[rows, :] = new
        final_ref[rows, :] = new

    over_rows(state.shape[0], finish)

    @pl.when(step == 0)
    def _():
        for copy in copies[6:]:
            copy.wait()

    @pl.when(step < RECURSIONS - 1)
    def _():
        attention_forward(state, bias_ref.at[0], cos_ref, sin_ref, gain_one[...], qkv_w,
                          n1_ref.at[0], q_ref.at[0], kz_ref.at[0], vz_ref.at[0], p_ref.at[0], o_ref.at[0])
        attention_out(state, o_ref.at[0], out_w, gain_two[...], attn, n2)


def finish_attention_backward(x_ref, gain, active_ref, du_ref, qkv_w, base, state, total, out_ref):
    total[...] = contract_last(du_ref[...], qkv_w[...])
    terms = jnp.zeros((1, state.shape[1]), F32)

    def lap(i, terms):
        rows = pl.ds(pl.multiple_of(i * ROWS, ROWS), ROWS)
        d_rows, term = norm_back(x_ref[rows, :], gain, total[rows, :])
        new = jnp.where(active_ref[rows, :] > 0, base[rows, :] + d_rows, state[rows, :])
        out_ref[rows, :] = new
        return terms + term

    return lax.fori_loop(0, state.shape[0] // ROWS, lap, terms)


def backward_steps(d_hidden_ref, active_ref, router_ref, cos_ref, sin_ref, gain_one, gain_two,
                   x_ref, a_ref, branch_ref, slope0, slope1, silu0, silu1, q_ref, kz_ref, vz_ref, p_ref,
                   qkv_hbm, out_hbm, *rest):
    feed_hbm, rest = rest[:6], rest[6:]
    (df_ref, dg0, dg1, dw0, dw1, d_attn_ref, du_ref, base_ref, state_ref, small_ref), rest = rest[:10], rest[10:]
    qkv_w, out_w, w0, w1, w2, w3, w4, w5, d_branch, total, do_ref, sems = rest
    step = pl.program_id(0)
    copies = load_all(list(zip(
        (feed_hbm[2], feed_hbm[0], feed_hbm[1], feed_hbm[5], feed_hbm[3], feed_hbm[4], out_hbm, qkv_hbm),
        (w2, w0, w1, w5, w3, w4, out_w, qkv_w))), sems)

    @pl.when(step == 0)
    def _():
        for copy in copies:
            copy.start()
        state_ref[...] = d_hidden_ref[...]
        small_ref[...] = jnp.zeros(small_ref.shape, F32)

    router_row = router_ref[pl.ds(RECURSIONS - 1 - step, 1), :]
    width = state_ref.shape[1]
    laps = state_ref.shape[0] // ROWS

    def enter(i, terms):
        rows = pl.ds(pl.multiple_of(i * ROWS, ROWS), ROWS)
        x = x_ref[0, rows, :]
        d_new = jnp.where(active_ref[0, rows, :] > 0, state_ref[rows, :], 0.0)
        gate = router_gate(x, router_row)
        d_gate = jnp.sum(d_new * branch_ref[0, rows, :], axis=-1, keepdims=True)
        d_logit = d_gate * gate * (1.0 - gate)
        spread = gate * d_new
        d_branch[rows, :] = spread
        df_ref[0, rows, :] = spread.astype(BF)
        base_ref[rows, :] = d_new + d_logit * router_row
        return terms + jnp.sum(d_logit * x, axis=0, keepdims=True)

    small_ref[pl.ds(2 + RECURSIONS - 1 - step, 1), :] = lax.fori_loop(0, laps, enter, jnp.zeros((1, width), F32))

    @pl.when(step == 0)
    def _():
        for copy in copies[:6]:
            copy.wait()

    feed_backward(df_ref.at[0], ((w0, w1, w2, slope0.at[0], silu0.at[0], dg0.at[0], dw0.at[0]),
                                 (w3, w4, w5, slope1.at[0], silu1.at[0], dg1.at[0], dw1.at[0])), total)

    def leave(i, terms):
        rows = pl.ds(pl.multiple_of(i * ROWS, ROWS), ROWS)
        d_after, term = norm_back(a_ref[0, rows, :], gain_two[...], total[rows, :].astype(BF).astype(F32))
        d_attn_ref[0, rows, :] = (d_branch[rows, :] + d_after).astype(BF)
        base_ref[rows, :] = base_ref[rows, :] + d_after
        return terms + term

    small_ref[1:2, :] = small_ref[1:2, :] + lax.fori_loop(0, laps, leave, jnp.zeros((1, width), F32))

    @pl.when(step == 0)
    def _():
        for copy in copies[6:]:
            copy.wait()

    @pl.when(step < RECURSIONS - 1)
    def _():
        attention_backward(d_attn_ref.at[0], out_w, qkv_w, cos_ref, sin_ref, q_ref.at[0], kz_ref.at[0], vz_ref.at[0],
                           p_ref.at[0], do_ref, du_ref.at[0])
        term = finish_attention_backward(x_ref.at[0], gain_one[...], active_ref.at[0], du_ref.at[0], qkv_w, base_ref, state_ref, total, state_ref)
        small_ref[0:1, :] = small_ref[0:1, :] + term


def last_attention(x_ref, active_ref, cos_ref, sin_ref, gain_one, q_ref, kz_ref, vz_ref, p_ref, d_attn_ref,
                   base_ref, state_ref, small_in, du_in, qkv_w, out_w, token, du_ref, d_input_ref, small_ref, do_ref, total):
    attention_backward(d_attn_ref.at[0], out_w, qkv_w, cos_ref, sin_ref, q_ref, kz_ref, vz_ref, p_ref, do_ref, du_ref.at[0])
    term = finish_attention_backward(x_ref.at[0], gain_one[...], active_ref.at[0], du_ref.at[0], qkv_w, base_ref, state_ref, total, d_input_ref)
    small_ref[...] = small_in[...]
    small_ref[0:1, :] = small_in[0:1, :] + term


def swap_dp(values_in, bit, n_dp):
    return lax.ppermute(values_in, "dp", [(i, i ^ (1 << bit)) for i in range(n_dp)])


def swap_mp(values_in):
    return lax.ppermute(values_in, "mp", [(0, 1), (1, 0)])


def halving(parts, order, n_dp, index):
    bits = n_dp.bit_length() - 1
    left = list(range(bits - 1, -1, -1))
    shape = parts.shape[1:]
    held = parts.reshape((2,) * bits + shape)
    for step, bit in enumerate(order):
        at = left.index(bit)
        upper = ((index >> bit) & 1) == 1
        low = lax.index_in_dim(held, 0, at, keepdims=False)
        high = lax.index_in_dim(held, 1, at, keepdims=False)
        keep, send = jnp.where(upper, high, low), jnp.where(upper, low, high)
        got = swap_dp(send, bit, n_dp)
        last = step == bits - 1
        total = keep.astype(F32) + got.astype(F32)
        held = total if last else total.astype(BF)
        left.remove(bit)
    return held


def orders_of(bits):
    rest = list(range(3, bits))
    if bits < 3:
        return [list(range(bits))] * 3
    return [[0, 1, 2] + rest, [1, 0, 2] + rest, [2, 0, 1] + rest]


PART = 2 * LANES
FFN_TILES = (4, 4, 2)
FFN_ORDERS = ((0, 1, 2, 3), (1, 0, 2, 3), (3, 2, 0, 1))
ATTN_ORDERS = ((0, 1, 3, 2), (2, 3, 1, 0))
SCHEDULE = (
    "T0", "T1", "T2", "A",
    "F0", "F1", "F2", "A0", "A1",
    "F0", "F1", "F2", "A0", "A1",
    "F0", "F1", "F2", "A0", "A1",
)
SMALL = 64


def halves(bit, outs, index):
    mine = (index >> bit) & 1
    inner = 1 << bit
    for out, which in zip(outs, (mine, 1 - mine)):
        for p in range(out.shape[0]):
            for q in range(inner):
                yield out, p, q, p * 2 * inner + which * inner + q


def ffn_terms(bit, tiles, n2_a, n2_b, df_a, df_b, dg_a, dg_b, dw_a, dw_b, m_a, m_b, token, keep_ref, send_ref, flat):
    width = n2_a.shape[1]
    part = tiles * LANES
    first = contract_rows(n2_a[...], jnp.concatenate([dg_a[...], dw_a[...]], axis=1))
    first = first + contract_rows(n2_b[...], jnp.concatenate([dg_b[...], dw_b[...]], axis=1))
    second = contract_rows(df_a[...], m_a[...]) + contract_rows(df_b[...], m_b[...])
    for matrix, (terms, at) in enumerate(((first, 0), (first, part), (second, 0))):
        for c in range(tiles):
            start = at + c * LANES
            flat[pl.ds(tiles * width * matrix + c, width, stride=tiles), :] = terms[:, start : start + LANES]
    rows = keep_ref.shape[2]
    for out, p, q, shard in halves(bit, (keep_ref, send_ref), lax.axis_index("dp")):
        out[p, q] = flat[pl.ds(pl.multiple_of(shard * rows, 8), rows), :].astype(BF)


def small_rows(small):
    rest = -small.shape[1] % LANES
    small = jnp.concatenate([small, jnp.zeros((small.shape[0], rest), F32)], axis=1)
    return jnp.concatenate([small[:, at : at + LANES] for at in range(0, small.shape[1], LANES)], axis=0)


def split_small(small, ref, start):
    high = small.astype(BF)
    ref[start : start + SMALL, :] = high
    ref[start + SMALL : start + 2 * SMALL, :] = (small - high.astype(F32)).astype(BF)


def rounded_small(small):
    high = small.astype(BF)
    return high.astype(F32) + (small - high.astype(F32)).astype(BF).astype(F32)


def joined_small(ref, start):
    return ref[start : start + SMALL, :].astype(F32) + ref[start + SMALL : start + 2 * SMALL, :].astype(F32)


def attn_terms(bits, cut, n1_a, n1_b, du_a, du_b, o_a, o_b, da_a, da_b, small_a, small_b, token,
               keep0, send0, keep1, send1, small_out, terms, flat):
    width = n1_a.shape[1]
    base = 0
    lower = lane_of(width // 2) < HEAD_DIM
    for lefts, rights in (((n1_a, n1_b), (du_a, du_b)), ((o_a, o_b), (da_a, da_b))):
        columns = rights[0].shape[1]
        half = columns // LANES
        for start in range(0, columns, PART):
            stop = min(columns, start + PART)
            block = sum(contract_rows(left[...], right[:, start:stop]) for left, right in zip(lefts, rights))
            if stop - start < PART:
                block = jnp.concatenate([block, jnp.zeros((width, PART - (stop - start)), F32)], axis=1)
            for part in range(0, stop - start, LANES):
                terms[(start + part) // LANES] = block[:, part : part + LANES]
        step = 2 * columns // LANES
        count = width // 2
        after = first_odd = None
        for c in range(half + 1):
            even = terms[c, pl.ds(0, count, stride=2), :]
            odd = other_half(terms[c, pl.ds(1, count, stride=2), :])
            if c < half:
                flat[pl.ds(base + c, count, stride=step), :] = even
            else:
                flat[pl.ds(base + c, count, stride=step), :] = jnp.where(lower, even, first_odd)
            if c == 0:
                first_odd = odd
            else:
                flat[pl.ds(base + half + c, count, stride=step), :] = jnp.where(lower, after, odd)
            after = odd
        base += width * columns // LANES
    index, core = lax.axis_index("dp"), lax.axis_index("mp")
    total = rounded_small(small_rows(small_a[...])) + rounded_small(small_rows(small_b[...]))
    small_out[...] = total
    shards, depth = 2 * keep0.shape[0] * keep0.shape[1], cut + keep1.shape[2]
    split_small(total, send0, shards // 2 * cut)

    def rows_of_shard(shard, low, high):
        start = pl.multiple_of((2 * shard + core) * depth + low, 8)
        return flat[pl.ds(start, high - low), :].astype(BF)

    mine = (index >> bits[0]) & 1
    inner = 1 << bits[0]
    for p in range(keep0.shape[0]):
        for q in range(inner):
            shard = 2 * p * inner + q
            keep0[p, q] = rows_of_shard(shard + mine * inner, 0, cut)
            at = (p * inner + q) * cut
            send0[at : at + cut, :] = rows_of_shard(shard + (1 - mine) * inner, 0, cut)
    for out, p, q, shard in halves(bits[1], (keep1, send1), index):
        out[p, q] = rows_of_shard(shard, cut, depth)


def fold(bit, kept, got, token, keep, send):
    mine = (lax.axis_index("dp") >> bit) & 1
    for p in range(kept.shape[0]):
        for q in range(kept.shape[2]):
            for out, which in ((keep, mine), (send, 1 - mine)):
                out[p, q] = (kept[p, which, q].astype(F32) + got[p, which, q].astype(F32)).astype(BF)


def fold_small(bit, kept, got, small, token, keep, send, small_out):
    mine = (lax.axis_index("dp") >> bit) & 1
    outer, _, inner, rows, _ = kept.shape
    for p in range(outer):
        for q in range(inner):
            totals = []
            for which in (mine, 1 - mine):
                start = pl.multiple_of(((2 * p + which) * inner + q) * rows, 16)
                totals.append((kept[p, which, q].astype(F32) + got[pl.ds(start, rows), :].astype(F32)).astype(BF))
            keep[p, q] = totals[0]
            at = (p * inner + q) * rows
            send[at : at + rows, :] = totals[1]
    total = rounded_small(small[...]) + joined_small(got, 2 * outer * inner * rows)
    small_out[...] = total
    split_small(total, send, outer * inner * rows)


def finish_streams(tiles, *refs):
    count = len(tiles)
    feeds, refs = refs[: 2 * count], refs[2 * count :]
    attn, refs = refs[:4], refs[4:]
    small, ffn_out, attn_out, small_out, flat = refs
    every = sum(tiles)
    rows = ffn_out.shape[0] // every
    base = 0
    for i, wide in enumerate(tiles):
        flat[: rows * wide, :] = feeds[2 * i][...].astype(F32) + feeds[2 * i + 1][...].astype(F32)
        for c in range(wide):
            ffn_out[pl.ds(base + c, rows, stride=every), :] = flat[pl.ds(c, rows, stride=wide), :]
        base += wide
    cut = attn[0].shape[0]
    attn_out[:cut, :] = attn[0][...].astype(F32) + attn[1][:cut, :].astype(F32)
    attn_out[cut:, :] = attn[2][...].astype(F32) + attn[3][...].astype(F32)
    total = rounded_small(small[...]) + joined_small(attn[1], cut)
    width = small_out.shape[1]
    for at in range(0, width, LANES):
        stop = min(width, at + LANES)
        small_out[:, at:stop] = total[at // LANES * 8 : at // LANES * 8 + 8, : stop - at]


class Stream:
    def __init__(self, order, bits):
        self.order, self.left, self.done = order, list(range(bits - 1, -1, -1)), 0
        self.kept = self.got = None

    def shape_for(self, array):
        at = self.left.index(self.order[self.done])
        rows, lanes = array.shape[-2:]
        return (1 << at, 2, 1 << (len(self.left) - 1 - at), rows, lanes)

    def sent(self, kept, send, n_dp):
        bit = self.order[self.done]
        self.kept, self.got = kept, swap_dp(send, bit, n_dp)
        self.left.remove(bit)
        self.done += 1


def on_device(
    hidden_in,
    sel_one,
    sel_two,
    sel_three,
    segment_ids,
    pad_mask,
    qkv_weight,
    out_weight,
    gate_weight,
    up_weight,
    down_weight,
    norm_one,
    norm_two,
    router_weight,
    d_hidden,
):
    seq_len, width = hidden_in.shape
    n_dp, n_mp = lax.axis_size("dp"), lax.axis_size("mp")
    dp_index, mp_index = lax.axis_index("dp"), lax.axis_index("mp")
    cosine, sine = rotary_tables(seq_len)
    weights = [(gate_weight, up_weight, down_weight)]
    weights.append(tuple(swap_mp(w) for w in weights[0]))
    gain_one, gain_two = norm_one.reshape(1, width), norm_two.reshape(1, width)
    padded = CHUNKS * LANES
    units = gate_weight.shape[1]
    feed_weights = (*weights[0], *weights[1])

    def shape(*dims, dtype=BF):
        return jax.ShapeDtypeStruct(dims, dtype)

    def whole(*dims, **kw):
        return pl.BlockSpec(dims, lambda *_: (0,) * len(dims), **kw)

    anywhere = pl.BlockSpec(memory_space=pl.ANY)
    one = pl.Buffered(1)
    stack = RECURSIONS, seq_len
    heads = (2 * KV_HEADS, seq_len, LANES)
    square = (HEADS, seq_len, seq_len)
    n1, q, kz, vz, p, o, attn, n2, bias, active = pl.pallas_call(
        first_attention,
        grid=(1,),
        in_specs=[
            whole(seq_len, width), *[whole(*ref.shape) for ref in (sel_one, sel_two, sel_three, segment_ids, pad_mask)],
            whole(seq_len, LANES), whole(seq_len, LANES), whole(1, width), whole(1, width), whole(*qkv_weight.shape), whole(*out_weight.shape),
        ],
        out_specs=[
            whole(1, seq_len, width), whole(seq_len, padded), whole(*heads), whole(*heads), whole(*square),
            whole(1, seq_len, width), whole(seq_len, width), whole(seq_len, width), whole(RECURSIONS, seq_len, seq_len), whole(*stack, 1),
        ],
        out_shape=[
            shape(*stack, width), shape(seq_len, padded), shape(*heads), shape(*heads), shape(*square),
            shape(*stack, width), shape(seq_len, width, dtype=F32), shape(seq_len, width),
            shape(*stack, seq_len, dtype=F32), shape(*stack, 1, dtype=F32),
        ],
        compiler_params=pltpu.CompilerParams(vmem_limit_bytes=VMEM_MIB * MIB),
        cost_estimate=pl.CostEstimate(flops=2 * 10**9, bytes_accessed=12 * 10**6, transcendentals=600000),
        name="first_attention",
    )(hidden_in, sel_one, sel_two, sel_three, segment_ids, pad_mask, cosine, sine, gain_one, gain_two, qkv_weight, out_weight)
    attention_0 = (q, kz, vz, p)

    def at_step(*dims):
        return pl.BlockSpec((1, *dims), lambda r: (r,) + (0,) * len(dims))

    def next_step(*dims):
        return pl.BlockSpec((1, *dims), lambda r: (jnp.minimum(r + 1, RECURSIONS - 1),) + (0,) * len(dims))

    def next_pair(*dims):
        return pl.BlockSpec((1, *dims), lambda r: (jnp.minimum(r, RECURSIONS - 2),) + (0,) * len(dims))

    weight_scratch = [pltpu.VMEM(w.shape, BF) for w in (qkv_weight, out_weight, *feed_weights)]
    results = pl.pallas_call(
        forward_steps,
        grid=(RECURSIONS,),
        in_specs=[
            whole(seq_len, width, pipeline_mode=one), whole(seq_len, width, pipeline_mode=one), whole(seq_len, width, pipeline_mode=one),
            next_step(seq_len, seq_len), at_step(seq_len, 1), whole(RECURSIONS, width),
            whole(seq_len, LANES), whole(seq_len, LANES), whole(1, width), whole(1, width),
            anywhere, anywhere, *[anywhere] * 8,
        ],
        out_specs=[
            next_step(seq_len, width), next_step(seq_len, width), next_pair(seq_len, padded), next_pair(*heads), next_pair(*heads),
            next_pair(*square), *[at_step(seq_len, width)] * 4, *[at_step(seq_len, units)] * 6, whole(seq_len, width),
        ],
        out_shape=[
            shape(*stack, width), shape(*stack, width), shape(RECURSIONS - 1, seq_len, padded), shape(RECURSIONS - 1, *heads), shape(RECURSIONS - 1, *heads),
            shape(RECURSIONS - 1, *square), *[shape(*stack, width, dtype=F32)] * 3, shape(*stack, width), *[shape(*stack, units)] * 6,
            shape(seq_len, width, dtype=F32),
        ],
        scratch_shapes=[
            *weight_scratch,
            pltpu.VMEM((seq_len, width), F32), pltpu.VMEM((seq_len, width), F32), pltpu.VMEM((seq_len, width), BF), pltpu.VMEM((seq_len, width), F32),
            pltpu.SemaphoreType.DMA((8,)),
        ],
        input_output_aliases={10: 0, 11: 1},
        compiler_params=pltpu.CompilerParams(vmem_limit_bytes=VMEM_MIB * MIB),
        cost_estimate=pl.CostEstimate(flops=12 * 10**9, bytes_accessed=50 * 10**6, transcendentals=4 * 10**6),
        name="forward_steps",
    )(hidden_in, attn, n2, bias, active, router_weight, cosine, sine, gain_one, gain_two, n1, o, qkv_weight, out_weight, *feed_weights)
    n1, o, q, kz, vz, p, x, a, branch, n2, m0, m1, slope0, slope1, silu0, silu1, state = results

    def back_step(*dims):
        return pl.BlockSpec((1, *dims), lambda i: (RECURSIONS - 1 - i,) + (0,) * len(dims))

    def back_pair(*dims):
        return pl.BlockSpec((1, *dims), lambda i: (jnp.maximum(RECURSIONS - 2 - i, 0),) + (0,) * len(dims))

    def back_next(*dims):
        return pl.BlockSpec((1, *dims), lambda i: (jnp.maximum(RECURSIONS - 1 - i, 1),) + (0,) * len(dims))

    results = pl.pallas_call(
        backward_steps,
        grid=(RECURSIONS,),
        in_specs=[
            whole(seq_len, width, pipeline_mode=one), back_step(seq_len, 1), whole(RECURSIONS, width),
            whole(seq_len, LANES), whole(seq_len, LANES), whole(1, width), whole(1, width),
            *[back_step(seq_len, width)] * 3, *[back_step(seq_len, units)] * 4,
            back_pair(seq_len, padded), back_pair(*heads), back_pair(*heads), back_pair(*square),
            *[anywhere] * 8,
        ],
        out_specs=[
            back_step(seq_len, width), *[back_step(seq_len, units)] * 4, back_step(seq_len, width), back_next(seq_len, qkv_weight.shape[1]),
            whole(seq_len, width), whole(seq_len, width), whole(8, width),
        ],
        out_shape=[
            shape(*stack, width), *[shape(*stack, units)] * 4, shape(*stack, width), shape(*stack, qkv_weight.shape[1]),
            shape(seq_len, width, dtype=F32), shape(seq_len, width, dtype=F32), shape(8, width, dtype=F32),
        ],
        scratch_shapes=[
            *weight_scratch,
            pltpu.VMEM((seq_len, width), F32), pltpu.VMEM((seq_len, width), F32), pltpu.VMEM((seq_len, padded), BF),
            pltpu.SemaphoreType.DMA((8,)),
        ],
        compiler_params=pltpu.CompilerParams(vmem_limit_bytes=VMEM_MIB * MIB),
        cost_estimate=pl.CostEstimate(flops=11 * 10**9, bytes_accessed=50 * 10**6, transcendentals=4 * 10**6),
        name="backward_steps",
    )(d_hidden, active, router_weight, cosine, sine, gain_one, gain_two, x, a, branch, slope0, slope1, silu0, silu1, q, kz, vz, p,
      qkv_weight, out_weight, *feed_weights)
    d_feed, dg0, dg1, dw0, dw1, d_attn, du, base, grad_state, small = results

    def run_last(token):
        return pl.pallas_call(
            last_attention,
            grid=(1,),
            in_specs=[
                whole(1, seq_len, width), whole(1, seq_len, 1), whole(seq_len, LANES), whole(seq_len, LANES), whole(1, width),
                whole(seq_len, padded), whole(*heads), whole(*heads), whole(*square), whole(1, seq_len, width),
                whole(seq_len, width), whole(seq_len, width), whole(8, width), anywhere, whole(*qkv_weight.shape), whole(*out_weight.shape), anywhere,
            ],
            out_specs=[whole(1, seq_len, qkv_weight.shape[1]), whole(seq_len, width), whole(8, width)],
            out_shape=[shape(*stack, qkv_weight.shape[1]), shape(seq_len, width, dtype=F32), shape(8, width, dtype=F32)],
            scratch_shapes=[pltpu.VMEM((seq_len, padded), BF), pltpu.VMEM((seq_len, width), F32)],
            input_output_aliases={13: 0},
            compiler_params=pltpu.CompilerParams(vmem_limit_bytes=VMEM_MIB * MIB),
            cost_estimate=pl.CostEstimate(flops=1, bytes_accessed=1, transcendentals=0),
            name="last_attention",
        )(x, active, cosine, sine, gain_one, *attention_0, d_attn, base, grad_state, small, du, qkv_weight, out_weight, token)

    def rows_of(stacked):
        return stacked.reshape(-1, stacked.shape[-1])

    two, feed = rows_of(n2), rows_of(d_feed)
    sides = ((dg0, dw0, m0), (dg1, dw1, m1))
    bits = n_dp.bit_length() - 1
    share = (qkv_weight.size + out_weight.size) // (n_dp * n_mp)
    if bits == 4 and 3 * width % n_dp == 0 and units == sum(FFN_TILES) * LANES and share % (8 * LANES) == 0:
        crossed = [(t, swap_mp(far)) for t, far in
                   ((n2, n2), (d_feed, d_feed), (dg0, dg1), (dw0, dw1), (m0, m1))]
        factors = [rows_of(t) for both in crossed for t in both]
        streams = [Stream(order, bits) for order in FFN_ORDERS]
        pair = [Stream(order, bits) for order in ATTN_ORDERS]
        depth = share // LANES
        cut = depth // 2 // 16 * 16
        common = dict(
            grid=(1,),
            compiler_params=pltpu.CompilerParams(vmem_limit_bytes=VMEM_MIB * MIB),
            cost_estimate=pl.CostEstimate(flops=1, bytes_accessed=1, transcendentals=0),
        )

        def wholes(arrays):
            return [whole(*t.shape) for t in arrays]

        def terms_of(j, token):
            stream, tiles = streams[j], FFN_TILES[j]
            at = sum(FFN_TILES[:j]) // tiles
            bit = stream.order[0]
            dims = (1 << (bits - 1 - bit), 1 << bit, 3 * width // n_dp * tiles, LANES)
            columns = pl.BlockSpec((factors[4].shape[0], tiles * LANES), lambda i: (0, at))
            keep, send = pl.pallas_call(
                functools.partial(ffn_terms, bit, tiles),
                in_specs=[*wholes(factors[:4]), *[columns] * 6, anywhere],
                out_specs=[whole(*dims)] * 2,
                out_shape=[shape(*dims)] * 2,
                scratch_shapes=[pltpu.VMEM((3 * width * tiles, LANES), F32)],
                name=f"ffn_terms_{j}",
                **common,
            )(*factors, token)
            stream.sent(keep, send, n_dp)
            return keep

        def fold_stream(stream, token, small_own=None):
            bit = stream.order[stream.done]
            dims = stream.shape_for(stream.kept)
            kept = stream.kept.reshape(dims)
            held = (dims[0], *dims[2:])
            if small_own is None:
                operands = (kept, stream.got.reshape(dims))
                outs = (shape(*held), shape(*held))
            else:
                operands = (kept, stream.got, small_own)
                outs = (shape(*held), shape(dims[0] * dims[2] * dims[3] + 2 * SMALL, LANES), shape(SMALL, LANES, dtype=F32))
            results = pl.pallas_call(
                functools.partial(fold if small_own is None else fold_small, bit),
                in_specs=[*wholes(operands), anywhere],
                out_specs=wholes(outs),
                out_shape=outs,
                name="fold_terms",
                **common,
            )(*operands, token)
            stream.sent(results[0], results[1], n_dp)
            return results

        du, grad_state, small = run_last(small)
        first_crossed = [(rows_of(n1), swap_mp(rows_of(n1))), (rows_of(du), swap_mp(rows_of(du)))]
        late_crossed = [(rows_of(o), swap_mp(rows_of(o))), (rows_of(d_attn), swap_mp(rows_of(d_attn))), (small, swap_mp(small))]
        token = small
        for item in SCHEDULE:
            if item[0] == "T":
                token = terms_of(int(item[1:]), token)
            elif item[0] == "F":
                token = fold_stream(streams[int(item[1:])], token)[0]
            elif item == "A":
                firsts = [t.order[0] for t in pair]
                dims = [(1 << (bits - 1 - bit), 1 << bit, rows, LANES) for bit, rows in zip(firsts, (cut, depth - cut))]
                operands = [t for both in (*first_crossed, *late_crossed) for t in both]
                outs = (shape(*dims[0]), shape(n_dp // 2 * cut + 2 * SMALL, LANES), shape(*dims[1]), shape(*dims[1]),
                        shape(SMALL, LANES, dtype=F32))
                keep0, send0, keep1, send1, small_own = pl.pallas_call(
                    functools.partial(attn_terms, tuple(firsts), cut),
                    in_specs=[*wholes(operands), anywhere],
                    out_specs=wholes(outs),
                    out_shape=outs,
                    scratch_shapes=[pltpu.VMEM((-(-du.shape[-1] // PART) * 2, width, LANES), F32),
                                    pltpu.VMEM((n_dp * 2 * depth, LANES), F32)],
                    name="attn_terms",
                    **common,
                )(*operands, token)
                pair[0].sent(keep0, send0, n_dp)
                pair[1].sent(keep1, send1, n_dp)
                token = small_own
            elif item == "A0":
                token, _, small_own = fold_stream(pair[0], token, small_own)
            else:
                token = fold_stream(pair[1], token)[0]
        ends = [t.reshape(t.shape[-2:]) for stream in (*streams, *pair) for t in (stream.kept, stream.got)]
        outs = (shape(3 * width // n_dp * sum(FFN_TILES), LANES, dtype=F32), shape(depth, LANES, dtype=F32), shape(*small.shape, dtype=F32))
        ffn_flat, attn_flat, small = pl.pallas_call(
            functools.partial(finish_streams, FFN_TILES),
            in_specs=wholes((*ends, small_own)),
            out_specs=wholes(outs),
            out_shape=outs,
            scratch_shapes=[pltpu.VMEM((3 * width // n_dp * max(FFN_TILES), LANES), F32)],
            name="finish_streams",
            **common,
        )(*ends, small_own)
        return (state, grad_state, attn_flat.reshape(-1), ffn_flat.reshape(1, -1), small[0], small[1], small[2 : 2 + RECURSIONS])

    du, grad_state, small = run_last(small)

    def side_terms(side, columns):
        return jnp.concatenate(
            [
                contract_rows(left, rows_of(sides[side][which])[:, columns]).astype(BF)
                for which, left in enumerate((two, two, feed))
            ],
            axis=0,
        )

    orders = orders_of(bits)
    if 3 * width % n_dp == 0 and units % 1280 == 0:
        fifth = units // 5
        streams = [(orders[i], slice(j * fifth, (j + 1) * fifth)) for i, j in ((0, 0), (1, 1), (2, 2), (0, 3), (1, 4))]
        done = []
        for order, columns in streams:
            terms = side_terms(0, columns).astype(F32) + swap_mp(side_terms(1, columns)).astype(F32)
            done.append(halving(terms.astype(BF).reshape(n_dp, 3 * width // n_dp, fifth), order, n_dp, dp_index))
        ffn_flat = jnp.concatenate(done, axis=1).reshape(1, -1)
    else:
        terms = side_terms(0, slice(None)).astype(F32) + swap_mp(side_terms(1, slice(None))).astype(F32)
        terms = terms.astype(BF).reshape(n_dp, 3 * width * units // n_dp // 128, 128)
        ffn_flat = halving(terms, orders[0], n_dp, dp_index).reshape(1, -1)

    grad_qkv = contract_rows(rows_of(n1), rows_of(du)).astype(BF)
    grad_out = contract_rows(rows_of(o), rows_of(d_attn)).astype(BF)
    attn = jnp.concatenate([grad_qkv.reshape(-1), grad_out.reshape(-1)]).reshape(n_dp, 2, share // 128, 128)
    keep = jnp.where(mp_index == 0, attn[:, 0], attn[:, 1])
    send = jnp.where(mp_index == 0, attn[:, 1], attn[:, 0])
    attn = (keep.astype(F32) + swap_mp(send).astype(F32)).astype(BF)
    cuts = [0, (share // 128) // 24 * 8, (share // 128) // 12 * 8, share // 128]
    attn_flat = jnp.concatenate(
        [halving(attn[:, a:b], order, n_dp, dp_index) for a, b, order in zip(cuts, cuts[1:], orders)], axis=0
    ).reshape(-1)

    small = small + swap_mp(small)
    for bit in range(bits):
        small = small + swap_dp(small, bit, n_dp)
    return (state, grad_state, attn_flat, ffn_flat, small[0], small[1], small[2 : 2 + RECURSIONS])


def solution(mesh):
    both = P(("dp", "mp"), None)
    in_specs = (
        both,
        both,
        both,
        both,
        both,
        both,
        P(),
        P(),
        P(None, "mp"),
        P(None, "mp"),
        P(None, "mp"),
        P(),
        P(),
        P(),
        both,
    )
    out_specs = (both, both, P(("dp", "mp")), P("mp", "dp"), P(), P(), P())
    return jax.shard_map(
        on_device, mesh=mesh, in_specs=in_specs, out_specs=out_specs, check_vma=False
    )
```

profile of v0, /device:TPU:0, one launch (start us, length us, event | category | flops | bytes accessed | tf_op | source)
XLA Modules:
  0.0 269.9 jit_solution(13693613663739631770)
XLA Ops:
  1.7 11.1 %first_attention.1 = (bf16[3,192,960]{2,1,0:T(8,128)(2,1)}, bf16[192,1024]{1,0:T(8,128)(2,1)}, bf16[10,192,128]{2,1,0:T(8,128)(2,1)}, bf16[10,192,128]{2,1,0:T(8...) custom-call(f32[192,960]{1,0:T(8,128)} %x0_ref.1, ...), custom_call_target="tpu_custom_call" | custom-call | flops 2000000000 | bytes 12000000 | tf_op jit(solution)/shard_map/first_attention/pallas_call | solution.py:655
  12.8 35.7 %forward_steps.1 = (bf16[3,192,960]{2,1,0:T(8,128)(2,1)}, bf16[3,192,960]{2,1,0:T(8,128)(2,1)}, bf16[2,192,1024]{2,1,0:T(8,128)(2,1)}, bf16[2,10,192,128]{3,2,1,...) custom-call(f32[192,960]{1,0:T(8,128)} %x0_ref.1, ...), custom_call_target="tpu_custom_call", output_to_operand_aliasing={{0}: (10, {}), {1}: (11, {})} | custom-call | flops 12000000000 | bytes 50000000 | tf_op jit(solution)/shard_map/forward_steps/pallas_call | solution.py:687
  48.9 52.7 %backward_steps.1 = (bf16[3,192,960]{2,1,0:T(8,128)(2,1)}, bf16[3,192,1280]{2,1,0:T(8,128)(2,1)}, bf16[3,192,1280]{2,1,0:T(8,128)(2,1)}, bf16[3,192,1280]{2,1,0:...) custom-call(f32[192,960]{1,0:T(8,128)} %d_hidden_ref.1, ...), custom_call_target="tpu_custom_call" | custom-call | flops 11000000512 | bytes 50000000 | tf_op jit(solution)/shard_map/backward_steps/pallas_call | solution.py:726
  102.8 12.3 %last_attention.1 = (bf16[3,192,1600]{2,1,0:T(8,128)(2,1)}, f32[192,960]{1,0:T(8,128)}, f32[8,960]{1,0:T(8,128)}) custom-call(f32[3,192,960]{2,1,0:T(8,128)} %get-tuple-element.101.x_ref, f32[3,192,1]{2,1,0:T(8,128)} %get-tuple-element.97.active_ref, f32[192,128]{1,0:T(8,128)} %constant.4.clone.cos_ref, ...), custom_call_target="tpu_custom_call", output_to_operand_aliasing={{0}: (13, {})} | custom-call | flops 1 | bytes 1 | tf_op jit(solution)/shard_map/last_attention/pallas_call | solution.py:757
  115.5 10.6 %ffn_terms_0.1 = (bf16[8,1,720,128]{3,2,1,0:T(8,128)(2,1)}, bf16[8,1,720,128]{3,2,1,0:T(8,128)(2,1)}) custom-call(bf16[576,960]{1,0:T(8,128)(2,1)} %bitcast.68, bf16[576,960]{1,0:T(8,128)(2,1)} %bitcast.3.n2_b, bf16[576,960]{1,0:T(8,128)(2,1)} %bitcast.71, bf16[576,960]{1,0:T(8,128)(2,1)} %bitcast.5.df_b, bf16[576,1280]{1,0:T(8,128)(2,1)} %bitcast.62, ...), custom_call_target="tpu_custom_call" | custom-call | flops 1 | bytes 1 | tf_op jit(solution)/shard_map/ffn_terms_0/pallas_call | solution.py:804
  126.1 2.7 %collective-permute-start.8 = (bf16[8,1,720,128]{3,2,1,0:T(8,128)(2,1)}, bf16[8,1,720,128]{3,2,1,0:T(8,128)(2,1)}, u32[]{:S(2)}, u32[]{:S(2)}) collective-permute-start(bf16[8,1,720,128]{3,2,1,0:T(8,128)(2,1)} %get-tuple-element.132), channel_id=1, source_target_pairs={{0,2},{2,0},{4,6},{6,4},{8,10},{10,8},{12,14},{14,12},{16,18},{18,... | collective-permute-start | bytes 4423688 | tf_op jit(solution)/shard_map/ppermute | solution.py:407
  128.8 10.5 %ffn_terms_1.1 = (bf16[4,2,720,128]{3,2,1,0:T(8,128)(2,1)}, bf16[4,2,720,128]{3,2,1,0:T(8,128)(2,1)}) custom-call(bf16[576,960]{1,0:T(8,128)(2,1)} %bitcast.69, bf16[576,960]{1,0:T(8,128)(2,1)} %bitcast.3.n2_b, bf16[576,960]{1,0:T(8,128)(2,1)} %bitcast.72, bf16[576,960]{1,0:T(8,128)(2,1)} %bitcast.5.df_b, bf16[576,1280]{1,0:T(8,128)(2,1)} %bitcast.63, ...), custom_call_target="tpu_custom_call" | custom-call | flops 1 | bytes 1 | tf_op jit(solution)/shard_map/ffn_terms_1/pallas_call | solution.py:804
  142.5 7.0 %ffn_terms_2.1 = (bf16[1,8,360,128]{3,2,1,0:T(8,128)(2,1)}, bf16[1,8,360,128]{3,2,1,0:T(8,128)(2,1)}) custom-call(bf16[576,960]{1,0:T(8,128)(2,1)} %bitcast.70, bf16[576,960]{1,0:T(8,128)(2,1)} %bitcast.3.n2_b, bf16[576,960]{1,0:T(8,128)(2,1)} %bitcast.73, bf16[576,960]{1,0:T(8,128)(2,1)} %bitcast.5.df_b, bf16[576,1280]{1,0:T(8,128)(2,1)} %bitcast.64, ...), custom_call_target="tpu_custom_call" | custom-call | flops 1 | bytes 1 | tf_op jit(solution)/shard_map/ffn_terms_2/pallas_call | solution.py:804
  149.5 2.6 collective-permute-start.17
  152.2 16.1 %attn_terms.1 = (bf16[8,1,288,128]{3,2,1,0:T(8,128)(2,1)}, bf16[2432,128]{1,0:T(8,128)(2,1)}, bf16[2,4,312,128]{3,2,1,0:T(8,128)(2,1)}, bf16[2,4,312,128]{3,2,1,0:T(8,128)(2,1)}, f32[64,128]{1,0:T(8,128)}) custom-call(bf16[576,960]{1,0:T(8,128)(2,1)} %bitcast.89, bf16[576,960]{1,0:T(8,128)(2,1)} %collective-permute-done.9.n1_b, bf16[576,1600]{1,0:T(8,128)(2,1)} %bitcast.75, ...), custom_call_target="tpu_custom_call" | custom-call | flops 1 | bytes 1 | tf_op jit(solution)/shard_map/attn_terms/pallas_call | solution.py:853
  168.3 3.3 %fold_terms.15 = (bf16[4,1,720,128]{3,2,1,0:T(8,128)(2,1)}, bf16[4,1,720,128]{3,2,1,0:T(8,128)(2,1)}) custom-call(bf16[4,2,1,720,128]{4,3,2,1,0:T(8,128)(2,1)} %bitcast.77, bf16[4,2,1,720,128]{4,3,2,1,0:T(8,128)(2,1)} %bitcast.13.got, f32[64,128]{1,0:T(8,128)} %get-tuple-element.138.token.small), custom_call_target="tpu_custom_call" | custom-call | flops 1 | bytes 1 | tf_op jit(solution)/shard_map/fold_terms/pallas_call | solution.py:827
  173.8 3.2 %fold_terms.16 = (bf16[4,1,720,128]{3,2,1,0:T(8,128)(2,1)}, bf16[4,1,720,128]{3,2,1,0:T(8,128)(2,1)}) custom-call(bf16[4,2,1,720,128]{4,3,2,1,0:T(8,128)(2,1)} %bitcast.76, bf16[4,2,1,720,128]{4,3,2,1,0:T(8,128)(2,1)} %bitcast.26.got, bf16[4,1,720,128]{3,2,1,0:T(8,128)(2,1)} %get-tuple-element.139.token), custom_call_target="tpu_custom_call" | custom-call | flops 1 | bytes 1 | tf_op jit(solution)/shard_map/fold_terms/pallas_call | solution.py:827
  180.6 4.6 %collective-permute-done.17 = bf16[1,8,360,128]{3,2,1,0:T(8,128)(2,1)} collective-permute-done((bf16[1,8,360,128]{3,2,1,0:T(8,128)(2,1)}, bf16[1,8,360,128]{3,2,1,0:T(8,128)(2,1)}, u32[]{:S(2)}, u32[]{:S(2)}) %collective-permute-start.17) | collective-permute-done | bytes 737312 | tf_op jit(solution)/shard_map/ppermute | solution.py:407
  185.3 2.4 fold_terms.17
  188.2 20.0 %collective-permute-done.16.got = bf16[2432,128]{1,0:T(8,128)(2,1)} collective-permute-done((bf16[2432,128]{1,0:T(8,128)(2,1)}, bf16[2432,128]{1,0:T(8,128)(2,1)}, u32[]{:S(2)}, u32[]{:S(2)}) %collective-permute-start.16) | collective-permute-done | bytes 622624 | tf_op jit(solution)/shard_map/ppermute | solution.py:407
  212.0 2.3 fold_terms.19
  214.2 2.5 collective-permute-start.20
  217.6 2.4 fold_terms.20
  221.6 2.3 fold_terms.21
  233.2 6.2 %collective-permute-done.19 = bf16[2,1,720,128]{3,2,0,1:T(8,128)(2,1)S(1)} collective-permute-done((bf16[2,1,720,128]{3,2,0,1:T(8,128)(2,1)}, bf16[2,1,720,128]{3,2,0,1:T(8,128)(2,1)S(1)}, u32[]{:S(2)}, u32[]{:S(2)}) %collective-permute-start.19) | collective-permute-done | bytes 368672 | tf_op jit(solution)/shard_map/ppermute | solution.py:407
  242.9 4.0 %collective-permute-done.25 = bf16[2,1,720,128]{3,2,0,1:T(8,128)(2,1)S(1)} collective-permute-done((bf16[2,1,720,128]{3,2,0,1:T(8,128)(2,1)}, bf16[2,1,720,128]{3,2,0,1:T(8,128)(2,1)S(1)}, u32[]{:S(2)}, u32[]{:S(2)}) %collective-permute-start.25) | collective-permute-done | bytes 368672 | tf_op jit(solution)/shard_map/ppermute | solution.py:407
  253.9 2.3 collective-permute-start.30
  259.5 4.0 %collective-permute-done.32 = bf16[1,1,312,128]{3,2,1,0:T(8,128)(2,1)S(1)} collective-permute-done((bf16[1,1,312,128]{3,2,1,0:T(8,128)(2,1)}, bf16[1,1,312,128]{3,2,1,0:T(8,128)(2,1)S(1)}, u32[]{:S(2)}, u32[]{:S(2)}) %collective-permute-start.32) | collective-permute-done | bytes 79904 | tf_op jit(solution)/shard_map/ppermute | solution.py:407
  264.4 2.5 finish_streams.1
  (90 shorter events, 45.6 us)
Async XLA Ops:
  48.5 54.1 %collective-permute-start.3 = (bf16[3,192,960]{2,1,0:T(8,128)(2,1)}, bf16[3,192,960]{2,1,0:T(8,128)(2,1)}, u32[]{:S(2)}, u32[]{:S(2)}) collective-permute-start(bf16[3,192,960]{2,1,0:T(8,128)(2,1)} %get-tuple-element.122), channel_id=1, source_target_pairs={{0,1},{1,0},{2,3},{3,2},{4,5},{5,4},{6,7},{7,6},{8,9},{9,8},{10,11... | collective-permute-start | bytes 3317768 | tf_op jit(solution)/shard_map/ppermute | solution.py:411
  101.5 14.0 %collective-permute-start.5 = (bf16[3,192,1280]{2,1,0:T(8,128)(2,1)}, bf16[3,192,1280]{2,1,0:T(8,128)(2,1)}, u32[]{:S(2)}, u32[]{:S(2)}) collective-permute-start(bf16[3,192,1280]{2,1,0:T(8,128)(2,1)} %get-tuple-element.125), channel_id=1, source_target_pairs={{0,1},{1,0},{2,3},{3,2},{4,5},{5,4},{6,7},{7,6},{8,9},{9,8},{10,11... | collective-permute-start | bytes 4423688 | tf_op jit(solution)/shard_map/ppermute | solution.py:411
  101.8 13.7 %collective-permute-start.6 = (bf16[3,192,1280]{2,1,0:T(8,128)(2,1)}, bf16[3,192,1280]{2,1,0:T(8,128)(2,1)}, u32[]{:S(2)}, u32[]{:S(2)}) collective-permute-start(bf16[3,192,1280]{2,1,0:T(8,128)(2,1)} %get-tuple-element.127), channel_id=1, source_target_pairs={{0,1},{1,0},{2,3},{3,2},{4,5},{5,4},{6,7},{7,6},{8,9},{9,8},{10,11... | collective-permute-start | bytes 4423688 | tf_op jit(solution)/shard_map/ppermute | solution.py:411
  102.1 13.4 %collective-permute-start.7 = (bf16[3,192,1280]{2,1,0:T(8,128)(2,1)}, bf16[3,192,1280]{2,1,0:T(8,128)(2,1)}, u32[]{:S(2)}, u32[]{:S(2)}) collective-permute-start(bf16[3,192,1280]{2,1,0:T(8,128)(2,1)} %get-tuple-element.129), channel_id=1, source_target_pairs={{0,1},{1,0},{2,3},{3,2},{4,5},{5,4},{6,7},{7,6},{8,9},{9,8},{10,11... | collective-permute-start | bytes 4423688 | tf_op jit(solution)/shard_map/ppermute | solution.py:411
  102.3 12.9 %collective-permute-start.4 = (bf16[3,192,960]{2,1,0:T(8,128)(2,1)}, bf16[3,192,960]{2,1,0:T(8,128)(2,1)}, u32[]{:S(2)}, u32[]{:S(2)}) collective-permute-start(bf16[3,192,960]{2,1,0:T(8,128)(2,1)} %get-tuple-element.123), channel_id=1, source_target_pairs={{0,1},{1,0},{2,3},{3,2},{4,5},{5,4},{6,7},{7,6},{8,9},{9,8},{10,11... | collective-permute-start | bytes 3317768 | tf_op jit(solution)/shard_map/ppermute | solution.py:411
  102.6 39.6 %collective-permute-start.9 = (bf16[576,960]{1,0:T(8,128)(2,1)}, bf16[576,960]{1,0:T(8,128)(2,1)}, u32[]{:S(2)}, u32[]{:S(2)}) collective-permute-start(bf16[576,960]{1,0:T(8,128)(2,1)} %bitcast.88), channel_id=1, source_target_pairs={{0,1},{1,0},{2,3},{3,2},{4,5},{5,4},{6,7},{7,6},{8,9},{9,8},{10,11... | collective-permute-start | bytes 3317768 | tf_op jit(solution)/shard_map/ppermute | solution.py:411
  115.1 37.0 %collective-permute-start.10 = (bf16[576,1600]{1,0:T(8,128)(2,1)}, bf16[576,1600]{1,0:T(8,128)(2,1)}, u32[]{:S(2)}, u32[]{:S(2)}) collective-permute-start(bf16[576,1600]{1,0:T(8,128)(2,1)} %bitcast.74), channel_id=1, source_target_pairs={{0,1},{1,0},{2,3},{3,2},{4,5},{5,4},{6,7},{7,6},{8,9},{9,8},{10,11... | collective-permute-start | bytes 5529608 | tf_op jit(solution)/shard_map/ppermute | solution.py:411
  126.1 42.2 %collective-permute-start.8 = (bf16[8,1,720,128]{3,2,1,0:T(8,128)(2,1)}, bf16[8,1,720,128]{3,2,1,0:T(8,128)(2,1)}, u32[]{:S(2)}, u32[]{:S(2)}) collective-permute-start(bf16[8,1,720,128]{3,2,1,0:T(8,128)(2,1)} %get-tuple-element.132), channel_id=1, source_target_pairs={{0,2},{2,0},{4,6},{6,4},{8,10},{10,8},{12,14},{14,12},{16,18},{18,... | collective-permute-start | bytes 4423688 | tf_op jit(solution)/shard_map/ppermute | solution.py:407
  139.3 34.5 %collective-permute-start.18 = (bf16[4,2,720,128]{3,2,1,0:T(8,128)(2,1)}, bf16[4,2,720,128]{3,2,1,0:T(8,128)(2,1)}, u32[]{:S(2)}, u32[]{:S(2)}) collective-permute-start(bf16[4,2,720,128]{3,2,1,0:T(8,128)(2,1)} %get-tuple-element.146), channel_id=1, source_target_pairs={{0,4},{2,6},{4,0},{6,2},{8,12},{10,14},{12,8},{14,10},{16,20},{18,... | collective-permute-start | bytes 4423688 | tf_op jit(solution)/shard_map/ppermute | solution.py:407
  149.5 35.7 %collective-permute-start.17 = (bf16[1,8,360,128]{3,2,1,0:T(8,128)(2,1)}, bf16[1,8,360,128]{3,2,1,0:T(8,128)(2,1)}, u32[]{:S(2)}, u32[]{:S(2)}) collective-permute-start(bf16[1,8,360,128]{3,2,1,0:T(8,128)(2,1)} %get-tuple-element.145), channel_id=1, source_target_pairs={{0,16},{2,18},{4,20},{6,22},{8,24},{10,26},{12,28},{14,30},{16,0},... | collective-permute-start | bytes 2211848 | tf_op jit(solution)/shard_map/ppermute | solution.py:407
  171.5 45.2 %collective-permute-start.14 = (bf16[4,1,720,128]{3,2,1,0:T(8,128)(2,1)}, bf16[4,1,720,128]{3,2,1,0:T(8,128)(2,1)S(1)}, u32[]{:S(2)}, u32[]{:S(2)}) collective-permute-start(bf16[4,1,720,128]{3,2,1,0:T(8,128)(2,1)} %get-tuple-element.140), channel_id=1, source_target_pairs={{0,4},{2,6},{4,0},{6,2},{8,12},{10,14},{12,8},{14,10},{16,20},{18,... | collective-permute-start | bytes 2211848 | tf_op jit(solution)/shard_map/ppermute | solution.py:407
  177.0 44.6 %collective-permute-start.23 = (bf16[4,1,720,128]{3,2,1,0:T(8,128)(2,1)}, bf16[4,1,720,128]{3,2,1,0:T(8,128)(2,1)}, u32[]{:S(2)}, u32[]{:S(2)}) collective-permute-start(bf16[4,1,720,128]{3,2,1,0:T(8,128)(2,1)} %get-tuple-element.157), channel_id=1, source_target_pairs={{0,2},{2,0},{4,6},{6,4},{8,10},{10,8},{12,14},{14,12},{16,18},{18,... | collective-permute-start | bytes 2211848 | tf_op jit(solution)/shard_map/ppermute | solution.py:407
  177.3 30.9 %collective-permute-start.16 = (bf16[2432,128]{1,0:T(8,128)(2,1)}, bf16[2432,128]{1,0:T(8,128)(2,1)}, u32[]{:S(2)}, u32[]{:S(2)}) collective-permute-start(bf16[2432,128]{1,0:T(8,128)(2,1)} %get-tuple-element.144), channel_id=1, source_target_pairs={{0,2},{2,0},{4,6},{6,4},{8,10},{10,8},{12,14},{14,12},{16,18},{18,... | collective-permute-start | bytes 1867784 | tf_op jit(solution)/shard_map/ppermute | solution.py:407
  179.1 32.9 %collective-permute-start.15 = (bf16[2,4,312,128]{3,2,1,0:T(8,128)(2,1)}, bf16[2,4,312,128]{3,2,1,0:T(8,128)(2,1)}, u32[]{:S(2)}, u32[]{:S(2)}) collective-permute-start(bf16[2,4,312,128]{3,2,1,0:T(8,128)(2,1)} %get-tuple-element.142), channel_id=1, source_target_pairs={{0,8},{2,10},{4,12},{6,14},{8,0},{10,2},{12,4},{14,6},{16,24},{18,... | collective-permute-start | bytes 1916936 | tf_op jit(solution)/shard_map/ppermute | solution.py:407
  187.6 36.8 %collective-permute-start.22 = (bf16[1,4,360,128]{3,2,1,0:T(8,128)(2,1)}, bf16[1,4,360,128]{3,2,1,0:T(8,128)(2,1)}, u32[]{:S(2)}, u32[]{:S(2)}) collective-permute-start(bf16[1,4,360,128]{3,2,1,0:T(8,128)(2,1)} %get-tuple-element.156), channel_id=1, source_target_pairs={{0,8},{2,10},{4,12},{6,14},{8,0},{10,2},{12,4},{14,6},{16,24},{18,... | collective-permute-start | bytes 1105928 | tf_op jit(solution)/shard_map/ppermute | solution.py:407
  210.4 16.4 %collective-permute-start.21 = (bf16[1280,128]{1,0:T(8,128)(2,1)}, bf16[1280,128]{1,0:T(8,128)(2,1)}, u32[]{:S(2)}, u32[]{:S(2)}) collective-permute-start(bf16[1280,128]{1,0:T(8,128)(2,1)} %get-tuple-element.154), channel_id=1, source_target_pairs={{0,4},{2,6},{4,0},{6,2},{8,12},{10,14},{12,8},{14,10},{16,20},{18,... | collective-permute-start | bytes 983048 | tf_op jit(solution)/shard_map/ppermute | solution.py:407
  214.2 15.9 %collective-permute-start.20 = (bf16[1,4,312,128]{3,2,1,0:T(8,128)(2,1)}, bf16[1,4,312,128]{3,2,1,0:T(8,128)(2,1)}, u32[]{:S(2)}, u32[]{:S(2)}) collective-permute-start(bf16[1,4,312,128]{3,2,1,0:T(8,128)(2,1)} %get-tuple-element.153), channel_id=1, source_target_pairs={{0,16},{2,18},{4,20},{6,22},{8,24},{10,26},{12,28},{14,30},{16,0},... | collective-permute-start | bytes 958472 | tf_op jit(solution)/shard_map/ppermute | solution.py:407
  220.0 19.5 %collective-permute-start.19 = (bf16[2,1,720,128]{3,2,0,1:T(8,128)(2,1)}, bf16[2,1,720,128]{3,2,0,1:T(8,128)(2,1)S(1)}, u32[]{:S(2)}, u32[]{:S(2)}) collective-permute-start(bf16[2,1,720,128]{3,2,0,1:T(8,128)(2,1)} %bitcast.117), channel_id=1, source_target_pairs={{0,8},{2,10},{4,12},{6,14},{8,0},{10,2},{12,4},{14,6},{16,24},{18,... | collective-permute-start | bytes 1105928 | tf_op jit(solution)/shard_map/ppermute | solution.py:407
  224.0 22.9 %collective-permute-start.25 = (bf16[2,1,720,128]{3,2,0,1:T(8,128)(2,1)}, bf16[2,1,720,128]{3,2,0,1:T(8,128)(2,1)S(1)}, u32[]{:S(2)}, u32[]{:S(2)}) collective-permute-start(bf16[2,1,720,128]{3,2,0,1:T(8,128)(2,1)} %bitcast.118), channel_id=1, source_target_pairs={{0,8},{2,10},{4,12},{6,14},{8,0},{10,2},{12,4},{14,6},{16,24},{18,... | collective-permute-start | bytes 1105928 | tf_op jit(solution)/shard_map/ppermute | solution.py:407
  226.3 23.5 %collective-permute-start.27 = (bf16[2,1,360,128]{3,2,0,1:T(8,128)(2,1)}, bf16[2,1,360,128]{3,2,0,1:T(8,128)(2,1)S(1)}, u32[]{:S(2)}, u32[]{:S(2)}) collective-permute-start(bf16[2,1,360,128]{3,2,0,1:T(8,128)(2,1)} %bitcast.120), channel_id=1, source_target_pairs={{0,2},{2,0},{4,6},{6,4},{8,10},{10,8},{12,14},{14,12},{16,18},{18,... | collective-permute-start | bytes 552968 | tf_op jit(solution)/shard_map/ppermute | solution.py:407
  228.8 23.4 %collective-permute-start.29 = (bf16[704,128]{1,0:T(8,128)(2,1)}, bf16[704,128]{1,0:T(8,128)(2,1)}, u32[]{:S(2)}, u32[]{:S(2)}) collective-permute-start(bf16[704,128]{1,0:T(8,128)(2,1)} %get-tuple-element.170), channel_id=1, source_target_pairs={{0,16},{2,18},{4,20},{6,22},{8,24},{10,26},{12,28},{14,30},{16,0},... | collective-permute-start | bytes 540680 | tf_op jit(solution)/shard_map/ppermute | solution.py:407
  232.0 25.2 %collective-permute-start.31 = (bf16[1,2,312,128]{3,2,1,0:T(8,128)(2,1)}, bf16[1,2,312,128]{3,2,1,0:T(8,128)(2,1)}, u32[]{:S(2)}, u32[]{:S(2)}) collective-permute-start(bf16[1,2,312,128]{3,2,1,0:T(8,128)(2,1)} %get-tuple-element.174), channel_id=1, source_target_pairs={{0,4},{2,6},{4,0},{6,2},{8,12},{10,14},{12,8},{14,10},{16,20},{18,... | collective-permute-start | bytes 479240 | tf_op jit(solution)/shard_map/ppermute | solution.py:407
  242.1 21.5 %collective-permute-start.24 = (bf16[1,1,720,128]{3,2,1,0:T(8,128)(2,1)}, bf16[1,1,720,128]{3,2,1,0:T(8,128)(2,1)S(1)}, u32[]{:S(2)}, u32[]{:S(2)}) collective-permute-start(bf16[1,1,720,128]{3,2,1,0:T(8,128)(2,1)} %get-tuple-element.163), channel_id=1, source_target_pairs={{0,16},{2,18},{4,20},{6,22},{8,24},{10,26},{12,28},{14,30},{16,0},... | collective-permute-start | bytes 552968 | tf_op jit(solution)/shard_map/ppermute | solution.py:407
  249.5 14.0 %collective-permute-start.26 = (bf16[1,1,720,128]{3,2,1,0:T(8,128)(2,1)}, bf16[1,1,720,128]{3,2,1,0:T(8,128)(2,1)S(1)}, u32[]{:S(2)}, u32[]{:S(2)}) collective-permute-start(bf16[1,1,720,128]{3,2,1,0:T(8,128)(2,1)} %get-tuple-element.166), channel_id=1, source_target_pairs={{0,16},{2,18},{4,20},{6,22},{8,24},{10,26},{12,28},{14,30},{16,0},... | collective-permute-start | bytes 552968 | tf_op jit(solution)/shard_map/ppermute | solution.py:407
  (20 other events, 101.6 us)
where the time goes:
time: 274 us; the launch traced here: 270 us
  Pallas kernels  191 us (70%)
  waiting for transfers between devices  43 us (16%)
  starting transfers between devices  28.4 us (10%)
  local copies, waits for them, and re-layouts  6.64 us (2%)
    pallas_call x1, Pallas kernels, on_device(): pl.pallas_call(backward_steps, grid=(RECURSIONS,), in_specs=[whole(seq_le...  52.7 us
    ppermute x20, waiting for transfers between devices, swap_dp(): lax.ppermute(values_in, 'dp', [(i, i ^ 1 << bit) for i in range(n_dp)])  41.7 us
    pallas_call x1, Pallas kernels, on_device(): pl.pallas_call(forward_steps, grid=(RECURSIONS,), in_specs=[whole(seq_len...  35.7 us
    pallas_call x15, Pallas kernels, fold_stream(): pl.pallas_call(functools.partial(fold if small_own is None else fold_smal...  32.6 us
    pallas_call x3, Pallas kernels, terms_of(): pl.pallas_call(functools.partial(ffn_terms, bit, tiles), in_specs=[*whole...  28 us
    ppermute x20, starting transfers between devices, swap_dp(): lax.ppermute(values_in, 'dp', [(i, i ^ 1 << bit) for i in range(n_dp)])  24.8 us
    pallas_call x1, Pallas kernels, on_device(): pl.pallas_call(functools.partial(attn_terms, tuple(firsts), cut), in_spec...  16.1 us
    pallas_call x1, Pallas kernels, run_last(): pl.pallas_call(last_attention, grid=(1,), in_specs=[whole(1, seq_len, wid...  12.3 us
  transfers between devices with their start and end apart: 33, of which 8 were waited for; matrix products, arithmetic and copies ran while one was open for 0% of the time, Pallas kernels for 57%

commit v1 on v0

--- a/solution.py
+++ b/solution.py
@@ -151,9 +151,10 @@
     over_rows(x_ref.shape[0], norm)
 
 
-def feed_forward(n2_ref, sides, f_ref):
+def feed_forward(n2_ref, sides, f_ref, ready):
     n2 = n2_ref[...]
     for side, (gate_w, up_w, down_w, m_ref, slope_ref, silu_ref) in enumerate(sides):
+        ready(3 * side, 3 * side + 1)
         for start in range(0, gate_w.shape[1], BLOCK):
             at = slice(start, start + BLOCK)
             g, u = plain(n2, gate_w[:, at]), plain(n2, up_w[:, at])
@@ -162,18 +163,21 @@
             m_ref[:, at] = (silu * u).astype(BF)
             slope_ref[:, at] = (u * s * (1.0 + g * (1.0 - s))).astype(BF)
             silu_ref[:, at] = silu.astype(BF)
+        ready(3 * side + 2)
         part = contract_last(m_ref[...], down_w[...])
         f_ref[...] = part if side == 0 else f_ref[...] + part
 
 
-def feed_backward(df_ref, sides, d_two_ref):
+def feed_backward(df_ref, sides, d_two_ref, ready):
     d_feed = df_ref[...]
     for side, (gate_w, up_w, down_w, slope_ref, silu_ref, dg_ref, du_ref) in enumerate(sides):
+        ready(3 * side)
         for start in range(0, gate_w.shape[1], BLOCK):
             at = slice(start, start + BLOCK)
             d_hidden = plain(d_feed, down_w[:, at])
             dg_ref[:, at] = (d_hidden * slope_ref[:, at].astype(F32)).astype(BF)
             du_ref[:, at] = (d_hidden * silu_ref[:, at].astype(F32)).astype(BF)
+        ready(3 * side + 1, 3 * side + 2)
         part = contract_last(dg_ref[...], gate_w[...]) + contract_last(du_ref[...], up_w[...])
         d_two_ref[...] = part if side == 0 else d_two_ref[...] + part
 
@@ -263,8 +267,17 @@
 
 
 def load_all(pairs, sems):
-    copies = [pltpu.make_async_copy(src, dst, sems.at[i]) for i, (src, dst) in enumerate(pairs)]
-    return copies
+    return [pltpu.make_async_copy(src, dst, sems.at[i]) for i, (src, dst) in enumerate(pairs)]
+
+
+def waits_at(condition, copies):
+    def ready(*which):
+        @pl.when(condition)
+        def _():
+            for i in which:
+                copies[i].wait()
+
+    return ready
 
 
 def forward_steps(x0_ref, attn0_ref, n20_ref, bias_ref, active_ref, router_ref, cos_ref, sin_ref, gain_one, gain_two,
@@ -283,11 +296,10 @@
         state[...] = x0_ref[...]
         attn[...] = attn0_ref[...]
         n2[...] = n20_ref[...]
-        for copy in copies[:6]:
-            copy.wait()
-
+
+    ready = waits_at(step == 0, copies)
     n2_ref[0] = n2[...]
-    feed_forward(n2, ((w0, w1, w2, m0.at[0], slope0.at[0], silu0.at[0]), (w3, w4, w5, m1.at[0], slope1.at[0], silu1.at[0])), total)
+    feed_forward(n2, ((w0, w1, w2, m0.at[0], slope0.at[0], silu0.at[0]), (w3, w4, w5, m1.at[0], slope1.at[0], silu1.at[0])), total, ready)
     router_row = router_ref[pl.ds(step, 1), :]
 
     def finish(rows):
@@ -301,11 +313,7 @@
         final_ref[rows, :] = new
 
     over_rows(state.shape[0], finish)
-
-    @pl.when(step == 0)
-    def _():
-        for copy in copies[6:]:
-            copy.wait()
+    ready(6, 7)
 
     @pl.when(step < RECURSIONS - 1)
     def _():
@@ -365,13 +373,9 @@
 
     small_ref[pl.ds(2 + RECURSIONS - 1 - step, 1), :] = lax.fori_loop(0, laps, enter, jnp.zeros((1, width), F32))
 
-    @pl.when(step == 0)
-    def _():
-        for copy in copies[:6]:
-            copy.wait()
-
+    ready = waits_at(step == 0, copies)
     feed_backward(df_ref.at[0], ((w0, w1, w2, slope0.at[0], silu0.at[0], dg0.at[0], dw0.at[0]),
-                                 (w3, w4, w5, slope1.at[0], silu1.at[0], dg1.at[0], dw1.at[0])), total)
+                                 (w3, w4, w5, slope1.at[0], silu1.at[0], dg1.at[0], dw1.at[0])), total, ready)
 
     def leave(i, terms):
         rows = pl.ds(pl.multiple_of(i * ROWS, ROWS), ROWS)
@@ -381,11 +385,7 @@
         return terms + term
 
     small_ref[1:2, :] = small_ref[1:2, :] + lax.fori_loop(0, laps, leave, jnp.zeros((1, width), F32))
-
-    @pl.when(step == 0)
-    def _():
-        for copy in copies[6:]:
-            copy.wait()
+    ready(6, 7)
 
     @pl.when(step < RECURSIONS - 1)
     def _():
@@ -395,10 +395,16 @@
         small_ref[0:1, :] = small_ref[0:1, :] + term
 
 
-def last_attention(x_ref, active_ref, cos_ref, sin_ref, gain_one, q_ref, kz_ref, vz_ref, p_ref, d_attn_ref,
-                   base_ref, state_ref, small_in, du_in, qkv_w, out_w, token, du_ref, d_input_ref, small_ref, do_ref, total):
+def last_attention(active_ref, cos_ref, sin_ref, gain_one, q_ref, kz_ref, vz_ref, p_ref, d_attn_ref, small_in, out_w,
+                   x_hbm, base_hbm, state_hbm, qkv_hbm, du_in, token, du_ref, d_input_ref, small_ref,
+                   do_ref, total, x, base, state, qkv_w, sems):
+    copies = load_all([(qkv_hbm, qkv_w), (x_hbm.at[0], x), (base_hbm, base), (state_hbm, state)], sems)
+    for copy in copies:
+        copy.start()
     attention_backward(d_attn_ref.at[0], out_w, qkv_w, cos_ref, sin_ref, q_ref, kz_ref, vz_ref, p_ref, do_ref, du_ref.at[0])
-    term = finish_attention_backward(x_ref.at[0], gain_one[...], active_ref.at[0], du_ref.at[0], qkv_w, base_ref, state_ref, total, d_input_ref)
+    for copy in copies:
+        copy.wait()
+    term = finish_attention_backward(x, gain_one[...], active_ref.at[0], du_ref.at[0], qkv_w, base, state, total, d_input_ref)
     small_ref[...] = small_in[...]
     small_ref[0:1, :] = small_in[0:1, :] + term
 
@@ -439,8 +445,8 @@
 
 PART = 2 * LANES
 FFN_TILES = (4, 4, 2)
-FFN_ORDERS = ((0, 1, 2, 3), (1, 0, 2, 3), (3, 2, 0, 1))
-ATTN_ORDERS = ((0, 1, 3, 2), (2, 3, 1, 0))
+FFN_ORDERS = ((0, 1, 2, 3), (2, 0, 1, 3), (1, 2, 3, 0))
+ATTN_ORDERS = ((0, 3, 2, 1), (3, 0, 1, 2))
 SCHEDULE = (
     "T0", "T1", "T2", "A",
     "F0", "F1", "F2", "A0", "A1",
@@ -459,16 +465,31 @@
                 yield out, p, q, p * 2 * inner + which * inner + q
 
 
-def ffn_terms(bit, tiles, n2_a, n2_b, df_a, df_b, dg_a, dg_b, dw_a, dw_b, m_a, m_b, token, keep_ref, send_ref, flat):
-    width = n2_a.shape[1]
-    part = tiles * LANES
-    first = contract_rows(n2_a[...], jnp.concatenate([dg_a[...], dw_a[...]], axis=1))
-    first = first + contract_rows(n2_b[...], jnp.concatenate([dg_b[...], dw_b[...]], axis=1))
-    second = contract_rows(df_a[...], m_a[...]) + contract_rows(df_b[...], m_b[...])
-    for matrix, (terms, at) in enumerate(((first, 0), (first, part), (second, 0))):
+def stacked_copies(pairs, sems):
+    flat_pairs = []
+    for sources, target in pairs:
+        rows = target.shape[0] // 2
+        flat_pairs += [(source, target.at[pl.ds(i * rows, rows)]) for i, source in enumerate(sources)]
+    copies = load_all(flat_pairs, sems)
+    for copy in copies:
+        copy.start()
+    return [copies[i : i + 2] for i in range(0, len(copies), 2)]
+
+
+def ffn_terms(bit, tiles, at, n2_a, n2_b, df_a, df_b, dg_a, dg_b, dw_a, dw_b, m_a, m_b, token, keep_ref, send_ref,
+              left, right, flat, sems):
+    width = left.shape[2]
+    columns = pl.ds(at, tiles * LANES)
+    parts = [tuple(ref.at[:, columns] for ref in both) for both in ((dg_a, dg_b), (dw_a, dw_b), (m_a, m_b))]
+    n2, dg, dw, df, m = stacked_copies(
+        [((n2_a, n2_b), left.at[0]), (parts[0], right.at[0]), (parts[1], right.at[1]),
+         ((df_a, df_b), left.at[1]), (parts[2], right.at[2])], sems)
+    for matrix, needed in enumerate((n2 + dg, dw, df + m)):
+        for copy in needed:
+            copy.wait()
+        terms = contract_rows(left[matrix // 2], right[matrix])
         for c in range(tiles):
-            start = at + c * LANES
-            flat[pl.ds(tiles * width * matrix + c, width, stride=tiles), :] = terms[:, start : start + LANES]
+            flat[pl.ds(tiles * width * matrix + c, width, stride=tiles), :] = terms[:, c * LANES : (c + 1) * LANES]
     rows = keep_ref.shape[2]
     for out, p, q, shard in halves(bit, (keep_ref, send_ref), lax.axis_index("dp")):
         out[p, q] = flat[pl.ds(pl.multiple_of(shard * rows, 8), rows), :].astype(BF)
@@ -496,16 +517,20 @@
 
 
 def attn_terms(bits, cut, n1_a, n1_b, du_a, du_b, o_a, o_b, da_a, da_b, small_a, small_b, token,
-               keep0, send0, keep1, send1, small_out, terms, flat):
-    width = n1_a.shape[1]
+               keep0, send0, keep1, send1, small_out, left, du_rows, da_rows, terms, flat, sems):
+    width = left.shape[2]
     base = 0
     lower = lane_of(width // 2) < HEAD_DIM
-    for lefts, rights in (((n1_a, n1_b), (du_a, du_b)), ((o_a, o_b), (da_a, da_b))):
-        columns = rights[0].shape[1]
+    n1, du, o, da = stacked_copies(
+        [((n1_a, n1_b), left.at[0]), ((du_a, du_b), du_rows), ((o_a, o_b), left.at[1]), ((da_a, da_b), da_rows)], sems)
+    for which, (right, needed) in enumerate(((du_rows, n1 + du), (da_rows, o + da))):
+        for copy in needed:
+            copy.wait()
+        columns = right.shape[1]
         half = columns // LANES
         for start in range(0, columns, PART):
             stop = min(columns, start + PART)
-            block = sum(contract_rows(left[...], right[:, start:stop]) for left, right in zip(lefts, rights))
+            block = contract_rows(left[which], right[:, start:stop])
             if stop - start < PART:
                 block = jnp.concatenate([block, jnp.zeros((width, PART - (stop - start)), F32)], axis=1)
             for part in range(0, stop - start, LANES):
@@ -577,7 +602,7 @@
     count = len(tiles)
     feeds, refs = refs[: 2 * count], refs[2 * count :]
     attn, refs = refs[:4], refs[4:]
-    small, ffn_out, attn_out, small_out, flat = refs
+    small, ffn_out, attn_out, one_out, two_out, router_out, flat = refs
     every = sum(tiles)
     rows = ffn_out.shape[0] // every
     base = 0
@@ -590,10 +615,13 @@
     attn_out[:cut, :] = attn[0][...].astype(F32) + attn[1][:cut, :].astype(F32)
     attn_out[cut:, :] = attn[2][...].astype(F32) + attn[3][...].astype(F32)
     total = rounded_small(small[...]) + joined_small(attn[1], cut)
-    width = small_out.shape[1]
+    width = one_out.shape[1]
     for at in range(0, width, LANES):
         stop = min(width, at + LANES)
-        small_out[:, at:stop] = total[at // LANES * 8 : at // LANES * 8 + 8, : stop - at]
+        tile = total[at // LANES * 8 : at // LANES * 8 + 8, : stop - at]
+        one_out[:, at:stop] = tile[0:1]
+        two_out[:, at:stop] = tile[1:2]
+        router_out[:, at:stop] = tile[2 : 2 + RECURSIONS]
 
 
 class Stream:
@@ -758,18 +786,21 @@
             last_attention,
             grid=(1,),
             in_specs=[
-                whole(1, seq_len, width), whole(1, seq_len, 1), whole(seq_len, LANES), whole(seq_len, LANES), whole(1, width),
+                whole(1, seq_len, 1), whole(seq_len, LANES), whole(seq_len, LANES), whole(1, width),
                 whole(seq_len, padded), whole(*heads), whole(*heads), whole(*square), whole(1, seq_len, width),
-                whole(seq_len, width), whole(seq_len, width), whole(8, width), anywhere, whole(*qkv_weight.shape), whole(*out_weight.shape), anywhere,
+                whole(8, width), whole(*out_weight.shape), *[anywhere] * 6,
             ],
             out_specs=[whole(1, seq_len, qkv_weight.shape[1]), whole(seq_len, width), whole(8, width)],
             out_shape=[shape(*stack, qkv_weight.shape[1]), shape(seq_len, width, dtype=F32), shape(8, width, dtype=F32)],
-            scratch_shapes=[pltpu.VMEM((seq_len, padded), BF), pltpu.VMEM((seq_len, width), F32)],
-            input_output_aliases={13: 0},
+            scratch_shapes=[
+                pltpu.VMEM((seq_len, padded), BF), *[pltpu.VMEM((seq_len, width), F32)] * 4,
+                pltpu.VMEM(qkv_weight.shape, BF), pltpu.SemaphoreType.DMA((4,)),
+            ],
+            input_output_aliases={15: 0},
             compiler_params=pltpu.CompilerParams(vmem_limit_bytes=VMEM_MIB * MIB),
             cost_estimate=pl.CostEstimate(flops=1, bytes_accessed=1, transcendentals=0),
             name="last_attention",
-        )(x, active, cosine, sine, gain_one, *attention_0, d_attn, base, grad_state, small, du, qkv_weight, out_weight, token)
+        )(active, cosine, sine, gain_one, *attention_0, d_attn, small, out_weight, x, base, grad_state, qkv_weight, du, token)
 
     def rows_of(stacked):
         return stacked.reshape(-1, stacked.shape[-1])
@@ -797,16 +828,17 @@
 
         def terms_of(j, token):
             stream, tiles = streams[j], FFN_TILES[j]
-            at = sum(FFN_TILES[:j]) // tiles
+            at = sum(FFN_TILES[:j]) * LANES
             bit = stream.order[0]
             dims = (1 << (bits - 1 - bit), 1 << bit, 3 * width // n_dp * tiles, LANES)
-            columns = pl.BlockSpec((factors[4].shape[0], tiles * LANES), lambda i: (0, at))
+            both = 2 * RECURSIONS * seq_len
             keep, send = pl.pallas_call(
-                functools.partial(ffn_terms, bit, tiles),
-                in_specs=[*wholes(factors[:4]), *[columns] * 6, anywhere],
+                functools.partial(ffn_terms, bit, tiles, at),
+                in_specs=[anywhere] * (len(factors) + 1),
                 out_specs=[whole(*dims)] * 2,
                 out_shape=[shape(*dims)] * 2,
-                scratch_shapes=[pltpu.VMEM((3 * width * tiles, LANES), F32)],
+                scratch_shapes=[pltpu.VMEM((2, both, width), BF), pltpu.VMEM((3, both, tiles * LANES), BF),
+                                pltpu.VMEM((3 * width * tiles, LANES), F32), pltpu.SemaphoreType.DMA((10,))],
                 name=f"ffn_terms_{j}",
                 **common,
             )(*factors, token)
@@ -852,11 +884,13 @@
                         shape(SMALL, LANES, dtype=F32))
                 keep0, send0, keep1, send1, small_own = pl.pallas_call(
                     functools.partial(attn_terms, tuple(firsts), cut),
-                    in_specs=[*wholes(operands), anywhere],
+                    in_specs=[*[anywhere] * 8, *wholes(operands[8:]), anywhere],
                     out_specs=wholes(outs),
                     out_shape=outs,
-                    scratch_shapes=[pltpu.VMEM((-(-du.shape[-1] // PART) * 2, width, LANES), F32),
-                                    pltpu.VMEM((n_dp * 2 * depth, LANES), F32)],
+                    scratch_shapes=[pltpu.VMEM((2, 2 * RECURSIONS * seq_len, width), BF),
+                                    *[pltpu.VMEM((2 * RECURSIONS * seq_len, t.shape[-1]), BF) for t in (du, d_attn)],
+                                    pltpu.VMEM((-(-du.shape[-1] // PART) * 2, width, LANES), F32),
+                                    pltpu.VMEM((n_dp * 2 * depth, LANES), F32), pltpu.SemaphoreType.DMA((8,))],
                     name="attn_terms",
                     **common,
                 )(*operands, token)
@@ -868,8 +902,9 @@
             else:
                 token = fold_stream(pair[1], token)[0]
         ends = [t.reshape(t.shape[-2:]) for stream in (*streams, *pair) for t in (stream.kept, stream.got)]
-        outs = (shape(3 * width // n_dp * sum(FFN_TILES), LANES, dtype=F32), shape(depth, LANES, dtype=F32), shape(*small.shape, dtype=F32))
-        ffn_flat, attn_flat, small = pl.pallas_call(
+        outs = (shape(3 * width // n_dp * sum(FFN_TILES), LANES, dtype=F32), shape(depth, LANES, dtype=F32),
+                shape(1, width, dtype=F32), shape(1, width, dtype=F32), shape(RECURSIONS, width, dtype=F32))
+        ffn_flat, attn_flat, one, two, router = pl.pallas_call(
             functools.partial(finish_streams, FFN_TILES),
             in_specs=wholes((*ends, small_own)),
             out_specs=wholes(outs),
@@ -878,7 +913,7 @@
             name="finish_streams",
             **common,
         )(*ends, small_own)
-        return (state, grad_state, attn_flat.reshape(-1), ffn_flat.reshape(1, -1), small[0], small[1], small[2 : 2 + RECURSIONS])
+        return (state, grad_state, attn_flat.reshape(-1), ffn_flat.reshape(1, -1), one.reshape(-1), two.reshape(-1), router)
 
     du, grad_state, small = run_last(small)
 

time: 274 us -> 262 us (0.956)
  waiting for transfers between devices: 43 us -> 35.3 us
  Pallas kernels: 191 us -> 185 us
  starting transfers between devices: 28.4 us -> 32.9 us
  local copies, waits for them, and re-layouts: 6.64 us -> 3.82 us
    ppermute x20, waiting for transfers between devices: 41.7 us -> 34 us  [swap_dp(): lax.ppermute(values_in, 'dp', [(i, i ^ 1 << bit) for i in range(n_dp)])]
    ppermute x20, starting transfers between devices: 24.8 us -> 29.3 us  [swap_dp(): lax.ppermute(values_in, 'dp', [(i, i ^ 1 << bit) for i in range(n_dp)])]
    pallas_call x4, Pallas kernels: 40.3 us -> 36.3 us  [the longest x3 23.8 us: terms_of(): pl.pallas_call(functools.partial(ffn_terms, bit, tiles, at), in_specs=[an...]
    slice x2 -> x0, local copies, waits for them, and re-layouts: 2.8 us -> none  [the longest x1 1.44 us: on_device(): small[1]]
  transfers between devices with their start and end apart: 33 -> 33, of which waited for: 8 -> 5; matrix products, arithmetic and copies ran while one was open for 0% -> 0% of each run, Pallas kernels for 57% -> 57%
where the time goes in v1:
time: 262 us; the launch traced here: 258 us
  Pallas kernels  185 us (71%)
  waiting for transfers between devices  35.3 us (13%)
  starting transfers between devices  32.9 us (13%)
  local copies, waits for them, and re-layouts  3.82 us (1%)
    pallas_call x1, Pallas kernels, on_device(): pl.pallas_call(backward_steps, grid=(RECURSIONS,), in_specs=[whole(seq_le...  52.5 us
    pallas_call x1, Pallas kernels, on_device(): pl.pallas_call(forward_steps, grid=(RECURSIONS,), in_specs=[whole(seq_len...  34.9 us
    ppermute x20, waiting for transfers between devices, swap_dp(): lax.ppermute(values_in, 'dp', [(i, i ^ 1 << bit) for i in range(n_dp)])  34 us
    pallas_call x15, Pallas kernels, fold_stream(): pl.pallas_call(functools.partial(fold if small_own is None else fold_smal...  32.6 us
    ppermute x20, starting transfers between devices, swap_dp(): lax.ppermute(values_in, 'dp', [(i, i ^ 1 << bit) for i in range(n_dp)])  29.3 us
    pallas_call x3, Pallas kernels, terms_of(): pl.pallas_call(functools.partial(ffn_terms, bit, tiles, at), in_specs=[an...  23.8 us
    pallas_call x1, Pallas kernels, on_device(): pl.pallas_call(functools.partial(attn_terms, tuple(firsts), cut), in_spec...  15.1 us
    pallas_call x1, Pallas kernels, run_last(): pl.pallas_call(last_attention, grid=(1,), in_specs=[whole(1, seq_len, 1),...  12.5 us
  transfers between devices with their start and end apart: 33, of which 5 were waited for; matrix products, arithmetic and copies ran while one was open for 0% of the time, Pallas kernels for 57%

profile of v1, /device:TPU:0, one launch (start us, length us, event | category | flops | bytes accessed | tf_op | source)
XLA Modules:
  0.0 258.0 jit_solution(5094238911836649158)
XLA Ops:
  1.7 11.1 %first_attention.1 = (bf16[3,192,960]{2,1,0:T(8,128)(2,1)}, bf16[192,1024]{1,0:T(8,128)(2,1)}, bf16[10,192,128]{2,1,0:T(8,128)(2,1)}, bf16[10,192,128]{2,1,0:T(8...) custom-call(f32[192,960]{1,0:T(8,128)} %x0_ref.1, ...), custom_call_target="tpu_custom_call" | custom-call | flops 2000000000 | bytes 12000000 | tf_op jit(solution)/shard_map/first_attention/pallas_call | solution.py:683
  12.8 34.9 %forward_steps.1 = (bf16[3,192,960]{2,1,0:T(8,128)(2,1)}, bf16[3,192,960]{2,1,0:T(8,128)(2,1)}, bf16[2,192,1024]{2,1,0:T(8,128)(2,1)}, bf16[2,10,192,128]{3,2,1,...) custom-call(f32[192,960]{1,0:T(8,128)} %x0_ref.1, ...), custom_call_target="tpu_custom_call", output_to_operand_aliasing={{0}: (10, {}), {1}: (11, {})} | custom-call | flops 12000000000 | bytes 50000000 | tf_op jit(solution)/shard_map/forward_steps/pallas_call | solution.py:715
  48.0 52.5 %backward_steps.1 = (bf16[3,192,960]{2,1,0:T(8,128)(2,1)}, bf16[3,192,1280]{2,1,0:T(8,128)(2,1)}, bf16[3,192,1280]{2,1,0:T(8,128)(2,1)}, bf16[3,192,1280]{2,1,0:...) custom-call(f32[192,960]{1,0:T(8,128)} %d_hidden_ref.1, ...), custom_call_target="tpu_custom_call" | custom-call | flops 11000000512 | bytes 50000000 | tf_op jit(solution)/shard_map/backward_steps/pallas_call | solution.py:754
  101.8 12.5 %last_attention.1 = (bf16[3,192,1600]{2,1,0:T(8,128)(2,1)}, f32[192,960]{1,0:T(8,128)}, f32[8,960]{1,0:T(8,128)}) custom-call(f32[3,192,1]{2,1,0:T(8,128)} %get-tuple-element.99.active_ref, f32[192,128]{1,0:T(8,128)} %constant.4.clone.cos_ref, f32[192,128]{1,0:T(8,128)} %constant.5.clone.sin_ref, ...), custom_call_target="tpu_custom_call", output_to_operand_aliasing={{0}: (15, {})} | custom-call | flops 1 | bytes 1 | tf_op jit(solution)/shard_map/last_attention/pallas_call | solution.py:785
  114.8 8.4 %ffn_terms_0.1 = (bf16[8,1,720,128]{3,2,1,0:T(8,128)(2,1)}, bf16[8,1,720,128]{3,2,1,0:T(8,128)(2,1)}) custom-call(bf16[576,960]{1,0:T(8,128)(2,1)} %bitcast.68, bf16[576,960]{1,0:T(8,128)(2,1)} %bitcast.3.n2_b, bf16[576,960]{1,0:T(8,128)(2,1)} %bitcast.71, bf16[576,960]{1,0:T(8,128)(2,1)} %bitcast.5.df_b, bf16[576,1280]{1,0:T(8,128)(2,1)} %bitcast.62, ...), custom_call_target="tpu_custom_call" | custom-call | flops 1 | bytes 1 | tf_op jit(solution)/shard_map/ffn_terms_0/pallas_call | solution.py:835
  123.2 2.8 %collective-permute-start.8 = (bf16[8,1,720,128]{3,2,1,0:T(8,128)(2,1)}, bf16[8,1,720,128]{3,2,1,0:T(8,128)(2,1)}, u32[]{:S(2)}, u32[]{:S(2)}) collective-permute-start(bf16[8,1,720,128]{3,2,1,0:T(8,128)(2,1)} %get-tuple-element.134), channel_id=1, source_target_pairs={{0,2},{2,0},{4,6},{6,4},{8,10},{10,8},{12,14},{14,12},{16,18},{18,... | collective-permute-start | bytes 4423688 | tf_op jit(solution)/shard_map/ppermute | solution.py:413
  125.9 8.4 %ffn_terms_1.1 = (bf16[2,4,720,128]{3,2,1,0:T(8,128)(2,1)}, bf16[2,4,720,128]{3,2,1,0:T(8,128)(2,1)}) custom-call(bf16[576,960]{1,0:T(8,128)(2,1)} %bitcast.69, bf16[576,960]{1,0:T(8,128)(2,1)} %bitcast.3.n2_b, bf16[576,960]{1,0:T(8,128)(2,1)} %bitcast.72, bf16[576,960]{1,0:T(8,128)(2,1)} %bitcast.5.df_b, bf16[576,1280]{1,0:T(8,128)(2,1)} %bitcast.63, ...), custom_call_target="tpu_custom_call" | custom-call | flops 1 | bytes 1 | tf_op jit(solution)/shard_map/ffn_terms_1/pallas_call | solution.py:835
  137.7 7.0 %ffn_terms_2.1 = (bf16[4,2,360,128]{3,2,1,0:T(8,128)(2,1)}, bf16[4,2,360,128]{3,2,1,0:T(8,128)(2,1)}) custom-call(bf16[576,960]{1,0:T(8,128)(2,1)} %bitcast.70, bf16[576,960]{1,0:T(8,128)(2,1)} %bitcast.3.n2_b, bf16[576,960]{1,0:T(8,128)(2,1)} %bitcast.73, bf16[576,960]{1,0:T(8,128)(2,1)} %bitcast.5.df_b, bf16[576,1280]{1,0:T(8,128)(2,1)} %bitcast.64, ...), custom_call_target="tpu_custom_call" | custom-call | flops 1 | bytes 1 | tf_op jit(solution)/shard_map/ffn_terms_2/pallas_call | solution.py:835
  146.3 15.1 %attn_terms.1 = (bf16[8,1,288,128]{3,2,1,0:T(8,128)(2,1)}, bf16[2432,128]{1,0:T(8,128)(2,1)}, bf16[1,8,312,128]{3,2,1,0:T(8,128)(2,1)}, bf16[1,8,312,128]{3,2,1,0:T(8,128)(2,1)}, f32[64,128]{1,0:T(8,128)}) custom-call(bf16[576,960]{1,0:T(8,128)(2,1)} %bitcast.89, bf16[576,960]{1,0:T(8,128)(2,1)} %collective-permute-done.9.n1_b, bf16[576,1600]{1,0:T(8,128)(2,1)} %bitcast.75, ...), custom_call_target="tpu_custom_call" | custom-call | flops 1 | bytes 1 | tf_op jit(solution)/shard_map/attn_terms/pallas_call | solution.py:885
  161.4 3.3 %fold_terms.15 = (bf16[4,1,720,128]{3,2,1,0:T(8,128)(2,1)}, bf16[4,1,720,128]{3,2,1,0:T(8,128)(2,1)}) custom-call(bf16[4,2,1,720,128]{4,3,2,1,0:T(8,128)(2,1)} %bitcast.77, bf16[4,2,1,720,128]{4,3,2,1,0:T(8,128)(2,1)} %bitcast.13.got, f32[64,128]{1,0:T(8,128)} %get-tuple-element.140.token.small), custom_call_target="tpu_custom_call" | custom-call | flops 1 | bytes 1 | tf_op jit(solution)/shard_map/fold_terms/pallas_call | solution.py:859
  165.2 3.8 %collective-permute-done.18 = bf16[2,4,720,128]{3,2,1,0:T(8,128)(2,1)} collective-permute-done((bf16[2,4,720,128]{3,2,1,0:T(8,128)(2,1)}, bf16[2,4,720,128]{3,2,1,0:T(8,128)(2,1)}, u32[]{:S(2)}, u32[]{:S(2)}) %collective-permute-start.18) | collective-permute-done | bytes 1474592 | tf_op jit(solution)/shard_map/ppermute | solution.py:413
  169.0 3.2 %fold_terms.16 = (bf16[4,1,720,128]{3,2,1,0:T(8,128)(2,1)}, bf16[4,1,720,128]{3,2,1,0:T(8,128)(2,1)}) custom-call(bf16[4,2,1,720,128]{4,3,2,1,0:T(8,128)(2,1)} %bitcast.76, bf16[4,2,1,720,128]{4,3,2,1,0:T(8,128)(2,1)} %bitcast.26.got, bf16[4,1,720,128]{3,2,1,0:T(8,128)(2,1)} %get-tuple-element.141.token), custom_call_target="tpu_custom_call" | custom-call | flops 1 | bytes 1 | tf_op jit(solution)/shard_map/fold_terms/pallas_call | solution.py:859
  174.3 2.6 %collective-permute-start.15 = (bf16[1,8,312,128]{3,2,1,0:T(8,128)(2,1)}, bf16[1,8,312,128]{3,2,1,0:T(8,128)(2,1)}, u32[]{:S(2)}, u32[]{:S(2)}) collective-permute-start(bf16[1,8,312,128]{3,2,1,0:T(8,128)(2,1)} %get-tuple-element.144), channel_id=1, source_target_pairs={{0,16},{2,18},{4,20},{6,22},{8,24},{10,26},{12,28},{14,30},{16,0},... | collective-permute-start | bytes 1916936 | tf_op jit(solution)/shard_map/ppermute | solution.py:413
  176.9 2.4 fold_terms.17
  180.8 22.7 %collective-permute-done.16.got = bf16[2432,128]{1,0:T(8,128)(2,1)} collective-permute-done((bf16[2432,128]{1,0:T(8,128)(2,1)}, bf16[2432,128]{1,0:T(8,128)(2,1)}, u32[]{:S(2)}, u32[]{:S(2)}) %collective-permute-start.16) | collective-permute-done | bytes 622624 | tf_op jit(solution)/shard_map/ppermute | solution.py:413
  203.5 2.2 fold_terms.18
  205.7 2.6 %collective-permute-start.21 = (bf16[1280,128]{1,0:T(8,128)(2,1)}, bf16[1280,128]{1,0:T(8,128)(2,1)}, u32[]{:S(2)}, u32[]{:S(2)}) collective-permute-start(bf16[1280,128]{1,0:T(8,128)(2,1)} %get-tuple-element.156), channel_id=1, source_target_pairs={{0,16},{2,18},{4,20},{6,22},{8,24},{10,26},{12,28},{14,30},{16,0},... | collective-permute-start | bytes 983048 | tf_op jit(solution)/shard_map/ppermute | solution.py:413
  208.3 2.3 fold_terms.19
  211.9 2.4 fold_terms.20
  215.8 2.4 fold_terms.21
  227.5 2.3 collective-permute-start.31
  229.8 3.9 %collective-permute-done.19 = bf16[2,1,720,128]{3,2,0,1:T(8,128)(2,1)S(1)} collective-permute-done((bf16[2,1,720,128]{3,2,0,1:T(8,128)(2,1)}, bf16[2,1,720,128]{3,2,0,1:T(8,128)(2,1)S(1)}, u32[]{:S(2)}, u32[]{:S(2)}) %collective-permute-start.19) | collective-permute-done | bytes 368672 | tf_op jit(solution)/shard_map/ppermute | solution.py:413
  250.8 3.6 %collective-permute-done.32 = bf16[1,1,312,128]{3,2,1,0:T(8,128)(2,1)S(1)} collective-permute-done((bf16[1,1,312,128]{3,2,1,0:T(8,128)(2,1)}, bf16[1,1,312,128]{3,2,1,0:T(8,128)(2,1)S(1)}, u32[]{:S(2)}, u32[]{:S(2)}) %collective-permute-start.32) | collective-permute-done | bytes 79904 | tf_op jit(solution)/shard_map/ppermute | solution.py:413
  255.3 2.5 finish_streams.1
  (88 shorter events, 42.4 us)
Async XLA Ops:
  47.7 53.9 %collective-permute-start.3 = (bf16[3,192,960]{2,1,0:T(8,128)(2,1)}, bf16[3,192,960]{2,1,0:T(8,128)(2,1)}, u32[]{:S(2)}, u32[]{:S(2)}) collective-permute-start(bf16[3,192,960]{2,1,0:T(8,128)(2,1)} %get-tuple-element.124), channel_id=1, source_target_pairs={{0,1},{1,0},{2,3},{3,2},{4,5},{5,4},{6,7},{7,6},{8,9},{9,8},{10,11... | collective-permute-start | bytes 3317768 | tf_op jit(solution)/shard_map/ppermute | solution.py:417
  100.5 14.2 %collective-permute-start.5 = (bf16[3,192,1280]{2,1,0:T(8,128)(2,1)}, bf16[3,192,1280]{2,1,0:T(8,128)(2,1)}, u32[]{:S(2)}, u32[]{:S(2)}) collective-permute-start(bf16[3,192,1280]{2,1,0:T(8,128)(2,1)} %get-tuple-element.127), channel_id=1, source_target_pairs={{0,1},{1,0},{2,3},{3,2},{4,5},{5,4},{6,7},{7,6},{8,9},{9,8},{10,11... | collective-permute-start | bytes 4423688 | tf_op jit(solution)/shard_map/ppermute | solution.py:417
  100.8 13.9 %collective-permute-start.6 = (bf16[3,192,1280]{2,1,0:T(8,128)(2,1)}, bf16[3,192,1280]{2,1,0:T(8,128)(2,1)}, u32[]{:S(2)}, u32[]{:S(2)}) collective-permute-start(bf16[3,192,1280]{2,1,0:T(8,128)(2,1)} %get-tuple-element.129), channel_id=1, source_target_pairs={{0,1},{1,0},{2,3},{3,2},{4,5},{5,4},{6,7},{7,6},{8,9},{9,8},{10,11... | collective-permute-start | bytes 4423688 | tf_op jit(solution)/shard_map/ppermute | solution.py:417
  101.1 13.7 %collective-permute-start.7 = (bf16[3,192,1280]{2,1,0:T(8,128)(2,1)}, bf16[3,192,1280]{2,1,0:T(8,128)(2,1)}, u32[]{:S(2)}, u32[]{:S(2)}) collective-permute-start(bf16[3,192,1280]{2,1,0:T(8,128)(2,1)} %get-tuple-element.131), channel_id=1, source_target_pairs={{0,1},{1,0},{2,3},{3,2},{4,5},{5,4},{6,7},{7,6},{8,9},{9,8},{10,11... | collective-permute-start | bytes 4423688 | tf_op jit(solution)/shard_map/ppermute | solution.py:417
  101.3 13.1 %collective-permute-start.4 = (bf16[3,192,960]{2,1,0:T(8,128)(2,1)}, bf16[3,192,960]{2,1,0:T(8,128)(2,1)}, u32[]{:S(2)}, u32[]{:S(2)}) collective-permute-start(bf16[3,192,960]{2,1,0:T(8,128)(2,1)} %get-tuple-element.125), channel_id=1, source_target_pairs={{0,1},{1,0},{2,3},{3,2},{4,5},{5,4},{6,7},{7,6},{8,9},{9,8},{10,11... | collective-permute-start | bytes 3317768 | tf_op jit(solution)/shard_map/ppermute | solution.py:417
  101.6 35.8 %collective-permute-start.9 = (bf16[576,960]{1,0:T(8,128)(2,1)}, bf16[576,960]{1,0:T(8,128)(2,1)}, u32[]{:S(2)}, u32[]{:S(2)}) collective-permute-start(bf16[576,960]{1,0:T(8,128)(2,1)} %bitcast.88), channel_id=1, source_target_pairs={{0,1},{1,0},{2,3},{3,2},{4,5},{5,4},{6,7},{7,6},{8,9},{9,8},{10,11... | collective-permute-start | bytes 3317768 | tf_op jit(solution)/shard_map/ppermute | solution.py:417
  114.4 31.9 %collective-permute-start.10 = (bf16[576,1600]{1,0:T(8,128)(2,1)}, bf16[576,1600]{1,0:T(8,128)(2,1)}, u32[]{:S(2)}, u32[]{:S(2)}) collective-permute-start(bf16[576,1600]{1,0:T(8,128)(2,1)} %bitcast.74), channel_id=1, source_target_pairs={{0,1},{1,0},{2,3},{3,2},{4,5},{5,4},{6,7},{7,6},{8,9},{9,8},{10,11... | collective-permute-start | bytes 5529608 | tf_op jit(solution)/shard_map/ppermute | solution.py:417
  123.2 38.3 %collective-permute-start.8 = (bf16[8,1,720,128]{3,2,1,0:T(8,128)(2,1)}, bf16[8,1,720,128]{3,2,1,0:T(8,128)(2,1)}, u32[]{:S(2)}, u32[]{:S(2)}) collective-permute-start(bf16[8,1,720,128]{3,2,1,0:T(8,128)(2,1)} %get-tuple-element.134), channel_id=1, source_target_pairs={{0,2},{2,0},{4,6},{6,4},{8,10},{10,8},{12,14},{14,12},{16,18},{18,... | collective-permute-start | bytes 4423688 | tf_op jit(solution)/shard_map/ppermute | solution.py:413
  134.4 34.6 %collective-permute-start.18 = (bf16[2,4,720,128]{3,2,1,0:T(8,128)(2,1)}, bf16[2,4,720,128]{3,2,1,0:T(8,128)(2,1)}, u32[]{:S(2)}, u32[]{:S(2)}) collective-permute-start(bf16[2,4,720,128]{3,2,1,0:T(8,128)(2,1)} %get-tuple-element.148), channel_id=1, source_target_pairs={{0,8},{2,10},{4,12},{6,14},{8,0},{10,2},{12,4},{14,6},{16,24},{18,... | collective-permute-start | bytes 4423688 | tf_op jit(solution)/shard_map/ppermute | solution.py:413
  144.7 32.1 %collective-permute-start.17 = (bf16[4,2,360,128]{3,2,1,0:T(8,128)(2,1)}, bf16[4,2,360,128]{3,2,1,0:T(8,128)(2,1)}, u32[]{:S(2)}, u32[]{:S(2)}) collective-permute-start(bf16[4,2,360,128]{3,2,1,0:T(8,128)(2,1)} %get-tuple-element.147), channel_id=1, source_target_pairs={{0,4},{2,6},{4,0},{6,2},{8,12},{10,14},{12,8},{14,10},{16,20},{18,... | collective-permute-start | bytes 2211848 | tf_op jit(solution)/shard_map/ppermute | solution.py:413
  164.7 46.3 %collective-permute-start.14 = (bf16[4,1,720,128]{3,2,1,0:T(8,128)(2,1)}, bf16[4,1,720,128]{3,2,1,0:T(8,128)(2,1)S(1)}, u32[]{:S(2)}, u32[]{:S(2)}) collective-permute-start(bf16[4,1,720,128]{3,2,1,0:T(8,128)(2,1)} %get-tuple-element.142), channel_id=1, source_target_pairs={{0,4},{2,6},{4,0},{6,2},{8,12},{10,14},{12,8},{14,10},{16,20},{18,... | collective-permute-start | bytes 2211848 | tf_op jit(solution)/shard_map/ppermute | solution.py:413
  172.2 43.6 %collective-permute-start.23 = (bf16[4,1,720,128]{3,2,1,0:T(8,128)(2,1)}, bf16[4,1,720,128]{3,2,1,0:T(8,128)(2,1)}, u32[]{:S(2)}, u32[]{:S(2)}) collective-permute-start(bf16[4,1,720,128]{3,2,1,0:T(8,128)(2,1)} %get-tuple-element.159), channel_id=1, source_target_pairs={{0,2},{2,0},{4,6},{6,4},{8,10},{10,8},{12,14},{14,12},{16,18},{18,... | collective-permute-start | bytes 2211848 | tf_op jit(solution)/shard_map/ppermute | solution.py:413
  172.6 30.9 %collective-permute-start.16 = (bf16[2432,128]{1,0:T(8,128)(2,1)}, bf16[2432,128]{1,0:T(8,128)(2,1)}, u32[]{:S(2)}, u32[]{:S(2)}) collective-permute-start(bf16[2432,128]{1,0:T(8,128)(2,1)} %get-tuple-element.146), channel_id=1, source_target_pairs={{0,2},{2,0},{4,6},{6,4},{8,10},{10,8},{12,14},{14,12},{16,18},{18,... | collective-permute-start | bytes 1867784 | tf_op jit(solution)/shard_map/ppermute | solution.py:413
  174.3 34.0 %collective-permute-start.15 = (bf16[1,8,312,128]{3,2,1,0:T(8,128)(2,1)}, bf16[1,8,312,128]{3,2,1,0:T(8,128)(2,1)}, u32[]{:S(2)}, u32[]{:S(2)}) collective-permute-start(bf16[1,8,312,128]{3,2,1,0:T(8,128)(2,1)} %get-tuple-element.144), channel_id=1, source_target_pairs={{0,16},{2,18},{4,20},{6,22},{8,24},{10,26},{12,28},{14,30},{16,0},... | collective-permute-start | bytes 1916936 | tf_op jit(solution)/shard_map/ppermute | solution.py:413
  179.2 40.5 %collective-permute-start.22 = (bf16[2,2,360,128]{3,2,1,0:T(8,128)(2,1)}, bf16[2,2,360,128]{3,2,1,0:T(8,128)(2,1)}, u32[]{:S(2)}, u32[]{:S(2)}) collective-permute-start(bf16[2,2,360,128]{3,2,1,0:T(8,128)(2,1)} %get-tuple-element.158), channel_id=1, source_target_pairs={{0,8},{2,10},{4,12},{6,14},{8,0},{10,2},{12,4},{14,6},{16,24},{18,... | collective-permute-start | bytes 1105928 | tf_op jit(solution)/shard_map/ppermute | solution.py:413
  205.7 16.3 %collective-permute-start.21 = (bf16[1280,128]{1,0:T(8,128)(2,1)}, bf16[1280,128]{1,0:T(8,128)(2,1)}, u32[]{:S(2)}, u32[]{:S(2)}) collective-permute-start(bf16[1280,128]{1,0:T(8,128)(2,1)} %get-tuple-element.156), channel_id=1, source_target_pairs={{0,16},{2,18},{4,20},{6,22},{8,24},{10,26},{12,28},{14,30},{16,0},... | collective-permute-start | bytes 983048 | tf_op jit(solution)/shard_map/ppermute | solution.py:413
  210.5 15.1 %collective-permute-start.20 = (bf16[4,1,312,128]{3,2,1,0:T(8,128)(2,1)}, bf16[4,1,312,128]{3,2,1,0:T(8,128)(2,1)}, u32[]{:S(2)}, u32[]{:S(2)}) collective-permute-start(bf16[4,1,312,128]{3,2,1,0:T(8,128)(2,1)} %get-tuple-element.155), channel_id=1, source_target_pairs={{0,2},{2,0},{4,6},{6,4},{8,10},{10,8},{12,14},{14,12},{16,18},{18,... | collective-permute-start | bytes 958472 | tf_op jit(solution)/shard_map/ppermute | solution.py:413
  214.3 19.4 %collective-permute-start.19 = (bf16[2,1,720,128]{3,2,0,1:T(8,128)(2,1)}, bf16[2,1,720,128]{3,2,0,1:T(8,128)(2,1)S(1)}, u32[]{:S(2)}, u32[]{:S(2)}) collective-permute-start(bf16[2,1,720,128]{3,2,0,1:T(8,128)(2,1)} %bitcast.115), channel_id=1, source_target_pairs={{0,8},{2,10},{4,12},{6,14},{8,0},{10,2},{12,4},{14,6},{16,24},{18,... | collective-permute-start | bytes 1105928 | tf_op jit(solution)/shard_map/ppermute | solution.py:413
  218.2 19.1 %collective-permute-start.25 = (bf16[2,1,720,128]{3,2,0,1:T(8,128)(2,1)}, bf16[2,1,720,128]{3,2,0,1:T(8,128)(2,1)S(1)}, u32[]{:S(2)}, u32[]{:S(2)}) collective-permute-start(bf16[2,1,720,128]{3,2,0,1:T(8,128)(2,1)} %bitcast.116), channel_id=1, source_target_pairs={{0,4},{2,6},{4,0},{6,2},{8,12},{10,14},{12,8},{14,10},{16,20},{18,... | collective-permute-start | bytes 1105928 | tf_op jit(solution)/shard_map/ppermute | solution.py:413
  221.7 20.2 %collective-permute-start.27 = (bf16[1,2,360,128]{3,2,1,0:T(8,128)(2,1)}, bf16[1,2,360,128]{3,2,1,0:T(8,128)(2,1)S(1)}, u32[]{:S(2)}, u32[]{:S(2)}) collective-permute-start(bf16[1,2,360,128]{3,2,1,0:T(8,128)(2,1)} %get-tuple-element.169), channel_id=1, source_target_pairs={{0,16},{2,18},{4,20},{6,22},{8,24},{10,26},{12,28},{14,30},{16,0},... | collective-permute-start | bytes 552968 | tf_op jit(solution)/shard_map/ppermute | solution.py:413
  223.9 20.4 %collective-permute-start.29 = (bf16[704,128]{1,0:T(8,128)(2,1)}, bf16[704,128]{1,0:T(8,128)(2,1)}, u32[]{:S(2)}, u32[]{:S(2)}) collective-permute-start(bf16[704,128]{1,0:T(8,128)(2,1)} %get-tuple-element.172), channel_id=1, source_target_pairs={{0,8},{2,10},{4,12},{6,14},{8,0},{10,2},{12,4},{14,6},{16,24},{18,... | collective-permute-start | bytes 540680 | tf_op jit(solution)/shard_map/ppermute | solution.py:413
  227.5 20.4 %collective-permute-start.31 = (bf16[2,1,312,128]{3,2,0,1:T(8,128)(2,1)}, bf16[2,1,312,128]{3,2,0,1:T(8,128)(2,1)}, u32[]{:S(2)}, u32[]{:S(2)}) collective-permute-start(bf16[2,1,312,128]{3,2,0,1:T(8,128)(2,1)} %bitcast.118), channel_id=1, source_target_pairs={{0,4},{2,6},{4,0},{6,2},{8,12},{10,14},{12,8},{14,10},{16,20},{18,... | collective-permute-start | bytes 479240 | tf_op jit(solution)/shard_map/ppermute | solution.py:413
  236.3 18.2 %collective-permute-start.24 = (bf16[1,1,720,128]{3,2,1,0:T(8,128)(2,1)}, bf16[1,1,720,128]{3,2,1,0:T(8,128)(2,1)S(1)}, u32[]{:S(2)}, u32[]{:S(2)}) collective-permute-start(bf16[1,1,720,128]{3,2,1,0:T(8,128)(2,1)} %get-tuple-element.165), channel_id=1, source_target_pairs={{0,16},{2,18},{4,20},{6,22},{8,24},{10,26},{12,28},{14,30},{16,0},... | collective-permute-start | bytes 552968 | tf_op jit(solution)/shard_map/ppermute | solution.py:413
  240.0 14.5 %collective-permute-start.26 = (bf16[1,1,720,128]{3,2,1,0:T(8,128)(2,1)}, bf16[1,1,720,128]{3,2,1,0:T(8,128)(2,1)S(1)}, u32[]{:S(2)}, u32[]{:S(2)}) collective-permute-start(bf16[1,1,720,128]{3,2,1,0:T(8,128)(2,1)} %get-tuple-element.168), channel_id=1, source_target_pairs={{0,16},{2,18},{4,20},{6,22},{8,24},{10,26},{12,28},{14,30},{16,0},... | collective-permute-start | bytes 552968 | tf_op jit(solution)/shard_map/ppermute | solution.py:413
  (20 other events, 97.4 us)
